TPU v7x, 512 devices: a whole 4x8x8 slice. The times are simulated.
512 devices in a mesh: grp: 2 (over core), row: 16 (over y, x_hi), col: 16 (over x_lo, z).
Axes of the slice: x: 4 (x_hi: 2, x_lo: 2; x = x_hi * 2 + x_lo), y: 8, z: 8, core: 2. Of those that a mesh axis runs over, the one named last changes fastest.
Arguments:
- density: float32 [256, 256, 256], P(('grp', 'row'), 'col'), may hold values from -8 to 8
- kernel_hat: float32 [512, 512, 512], P(('grp', 'row'), 'col'), may hold values from 0 to 8193, as said below
Outputs:
- potential: float32 [256, 256, 256], P(('grp', 'row'), 'col')
Inputs may be any that keep to these rules, and one draw needn't show every extreme that they name: kernel_hat[b, c, a] is unchanged when any one of its three indices i is replaced by (512 - i) mod 512.
All inputs are finite; a program needn't handle non-finite values.
Results may differ from a plain program's by a relative error of at most 0.000051.
Values sent between devices are 32-bit elements; how exact they have to be, the bound alone decides.
No kernel may reach another device: no remote copies, remote signals or barrier semaphores. Data moves between devices by JAX's collectives and lax.ppermute only.
A program may use at most 64 MiB of HBM per device.

v0:
```python
import functools

import jax
import jax.numpy as jnp
import ml_dtypes
import numpy as np
from jax import lax
from jax.experimental import pallas as pl
from jax.experimental.pallas import tpu as pltpu
from jax.sharding import PartitionSpec as P


GA = ("grp", "row")
ALL = ("col", "grp", "row")
NN = (((1,), (0,)), ((), ()))
NT = (((1,), (1,)), ((), ()))
VMEM = pl.BlockSpec(memory_space=pltpu.VMEM)


def modes(freqs_c, freqs_s, cells, length):
    centre = np.arange(cells) - (cells - 1) / 2.0
    angle = 2.0 * np.pi / length
    return np.concatenate(
        [np.cos(angle * np.outer(freqs_c, centre)), np.sin(angle * np.outer(freqs_s, centre))], 0
    )


def halves(table):
    table = np.asarray(table, np.float32)
    hi = table.astype(ml_dtypes.bfloat16)
    lo = (table - hi.astype(np.float32)).astype(ml_dtypes.bfloat16)
    return jnp.asarray(hi), jnp.asarray(lo)


def split(x):
    hi = x.astype(jnp.bfloat16)
    return hi, (x - hi.astype(jnp.float32)).astype(jnp.bfloat16)


def dot3(left, right, dims):
    one = functools.partial(lax.dot_general, dimension_numbers=dims, preferred_element_type=jnp.float32)
    return one(left[0], right[0]) + (one(left[0], right[1]) + one(left[1], right[0]))


def exchange_blocks(v, block):
    count, lanes = len(v), v[0].shape[1]
    lane_block = lax.broadcasted_iota(jnp.int32, v[0].shape, 1) // block
    step = 1
    while step < count:
        odd = (lane_block & step) != 0
        w = list(v)
        for n in range(count):
            if n & step == 0:
                low, high = v[n], v[n + step]
                w[n] = jnp.where(odd, pltpu.roll(high, step * block, 1), low)
                w[n + step] = jnp.where(odd, high, pltpu.roll(low, lanes - step * block, 1))
        v = w
        step *= 2
    return v


def forward_z(d_ref, th_ref, tl_ref, out_ref):
    d = d_ref[...]
    d = d.reshape(d.shape[0] * d.shape[1], d.shape[2])
    out_ref[...] = dot3((th_ref[...], tl_ref[...]), split(d), NT)


def pick_kernel(k_ref, out_ref, *, blocks_a, half):
    index = lax.axis_index("grp") * lax.axis_size("row") + lax.axis_index("row")
    first = jnp.where(index >= blocks_a // 2, 1, 0)
    rows = out_ref.shape[1]
    edge = k_ref[0]
    pieces = []
    for t in range(half // 64 + 1):
        tile = edge[:, t // 2 * 128 : t // 2 * 128 + 128]
        pieces.append(tile if t % 2 else pltpu.roll(tile, 64, 1))
    for s in range(rows):
        row = k_ref[first + s]
        out_ref[:, s, :half] = row[:, :half]
        last = row[:, half:]
        if s < len(pieces):
            lane = lax.broadcasted_iota(jnp.int32, last.shape, 1)
            last = jnp.where(lane < 64, last, pieces[s])
        out_ref[:, s, half:] = last


def convolve(r_ref, k_ref, bh_ref, bl_ref, ah_ref, al_ref, out_ref, *, blocks_a, blocks_b, slab_x, slab_y):
    cells = blocks_b * slab_y
    half = cells
    per = slab_x
    groups = []
    for h in range(blocks_b // per):
        v = [r_ref[(h * per + n) * blocks_a : (h * per + n + 1) * blocks_a, :] for n in range(per)]
        groups.append(jnp.concatenate(exchange_blocks(v, slab_y), 0))
    r = jnp.concatenate(groups, 1)
    tb = (bh_ref[...], bl_ref[...])
    ta = (ah_ref[...], al_ref[...])
    p = dot3(tb, split(r), NT)
    q = dot3(split(p), ta, NN)
    k = k_ref[...]
    k = k.reshape(k.shape[0] * k.shape[1], k.shape[2])
    main = k[:, :half]
    column = k[:, half : half + 1]
    tile = k_ref[blocks_a // 2][:, half:]
    lane = lax.broadcasted_iota(jnp.int32, (1, 128), 1)
    parts = []
    for t in range(0, half // 64, 2):
        parts.append(jnp.where(lane < 64, pltpu.roll(tile[t : t + 1], 64, 1), tile[t + 1 : t + 2]))
    row = jnp.concatenate(parts, 1)
    corner = tile[half // 64 : half // 64 + 1, 64:65]
    row_id = lax.broadcasted_iota(jnp.int32, main.shape, 0)
    lane_id = lax.broadcasted_iota(jnp.int32, main.shape, 1)
    first_row, first_lane = row_id == 0, lane_id == 0
    scale = jnp.where(first_row, 0.5, 1.0) * jnp.where(first_lane, 0.5, 1.0) * (1.0 / (half * half))
    cc = main
    cs = jnp.where(first_lane, column, main)
    sc = jnp.where(first_row, row, main)
    ss = jnp.where(first_lane, column, main)
    ss = jnp.where(first_row, jnp.where(first_lane, corner, row), ss)
    kk = jnp.concatenate(
        [jnp.concatenate([cc * scale, cs * scale], 1), jnp.concatenate([sc * scale, ss * scale], 1)], 0
    )
    w = dot3(ta, split(q * kk), NT)
    v = dot3(split(w), tb, NN)
    for h in range(blocks_b // per):
        lanes = slice(h * per * slab_y, (h + 1) * per * slab_y)
        v_h = exchange_blocks([v[n * blocks_a : (n + 1) * blocks_a, lanes] for n in range(per)], slab_y)
        for n in range(per):
            out_ref[(h * per + n) * blocks_a : (h * per + n + 1) * blocks_a, :] = v_h[n]


def inverse_z(r_ref, th_ref, tl_ref, out_ref):
    r = r_ref[...]
    modes_c = r.shape[0] // 2
    row_id = lax.broadcasted_iota(jnp.int32, r.shape, 0)
    r = r * jnp.where(row_id % modes_c == 0, 0.5 / modes_c, 1.0 / modes_c)
    out = dot3(split(r.T), (th_ref[...], tl_ref[...]), NN)
    out_ref[...] = out.reshape(out_ref.shape)


def call(kernel, shape, operands, flops):
    size = sum(x.size * x.dtype.itemsize for x in operands) + 4 * int(np.prod(shape))
    return pl.pallas_call(
        kernel,
        out_shape=jax.ShapeDtypeStruct(shape, jnp.float32),
        in_specs=[VMEM] * len(operands),
        out_specs=VMEM,
        compiler_params=pltpu.CompilerParams(vmem_limit_bytes=40 * 1024 * 1024),
        cost_estimate=pl.CostEstimate(flops=flops, bytes_accessed=size, transcendentals=0),
    )(*operands)


def body(density, kernel_hat):
    blocks_a = lax.axis_size(GA)
    blocks_b = lax.axis_size("col")
    slab_x, slab_y, cells = density.shape
    length = 2 * cells
    per_b, per_c = kernel_hat.shape[:2]

    tz = halves(modes(np.arange(cells), cells - np.arange(cells), cells, length))
    owner, sub = np.divmod(np.arange(cells), cells // blocks_a)
    order_b = np.where(owner < blocks_a // 2, per_b * owner + sub, length - 1 - per_b * owner - sub)
    tb = halves(modes(order_b, np.where(order_b == 0, cells, order_b), cells, length))
    order_a = np.arange(cells)
    order_x = np.arange(cells).reshape(blocks_a, slab_x).T.reshape(-1)
    ta = halves(modes(order_a, np.where(order_a == 0, cells, order_a), cells, length)[:, order_x].T)

    picked = pl.pallas_call(
        functools.partial(pick_kernel, blocks_a=blocks_a, half=cells),
        grid=(1,),
        out_shape=jax.ShapeDtypeStruct((per_c, cells // blocks_a, cells + 128), jnp.float32),
        in_specs=[pl.BlockSpec((cells // blocks_a + 1, per_c, cells + 128), lambda i: (0, 0, 0))],
        out_specs=pl.BlockSpec((per_c, cells // blocks_a, cells + 128), lambda i: (0, 0, 0)),
        cost_estimate=pl.CostEstimate(flops=0, bytes_accessed=8 * 32 * 8 * 384, transcendentals=0),
    )(kernel_hat)
    kernel = lax.all_to_all(picked, GA, split_axis=0, concat_axis=0, tiled=True)

    sent = call(forward_z, (length, slab_x * slab_y), (density, *tz), 6 * 128 * 256 * 512)
    got = lax.all_to_all(sent, ALL, split_axis=0, concat_axis=0, tiled=True)
    sizes = dict(blocks_a=blocks_a, blocks_b=blocks_b, slab_x=slab_x, slab_y=slab_y)
    back = call(
        functools.partial(convolve, **sizes),
        (length, slab_x * slab_y),
        (got, kernel, *tb, *ta),
        6 * 200 * 10**6,
    )
    got = lax.all_to_all(back, ALL, split_axis=0, concat_axis=0, tiled=True)
    return call(inverse_z, density.shape, (got, *tz), 6 * 128 * 256 * 512)


def solution(mesh):
    return jax.shard_map(
        body,
        mesh=mesh,
        in_specs=(P(GA, "col", None), P(GA, "col", None)),
        out_specs=P(GA, "col", None),
        check_vma=False,
    )
```

profile of v0, /device:TPU:1, one launch (start us, length us, event | category | flops | bytes accessed | tf_op | source)
XLA Modules:
  0.0 93.0 jit_solution(12270605108418265285)
XLA Ops:
  0.0 0.0 copy-start
  0.0 0.9 %copy-done = bf16[512,256]{1,0:T(8,128)(2,1)S(1)} copy-done((bf16[512,256]{1,0:T(8,128)(2,1)S(1)}, bf16[512,256]{1,0:T(8,128)(2,1)}, u32[]{:S(2)}) %copy-start) | copy-done | bytes 262168
  1.0 0.0 copy-start.2
  1.0 0.9 %copy-done.2 = bf16[512,256]{1,0:T(8,128)(2,1)S(1)} copy-done((bf16[512,256]{1,0:T(8,128)(2,1)S(1)}, bf16[512,256]{1,0:T(8,128)(2,1)}, u32[]{:S(2)}) %copy-start.2) | copy-done | bytes 262168
  1.9 0.0 copy-start.4
  1.9 0.9 copy-done.4
  2.8 1.1 %shard_map.82 = f32[512,128]{1,0:T(8,128)} custom-call(f32[8,16,256]{2,1,0:T(8,128)S(1)} %copy-done.4, bf16[512,256]{1,0:T(8,128)(2,1)S(1)} %copy-done, bf16[512,256]{1,0:T(8,128)(2,1)S(1)} %copy-done.2), custom_call_target="tpu_custom_call" | custom-call | flops 100663296 | bytes 917504 | tf_op jit(solution)/shard_map/pallas_call | solution.py:143
  3.9 22.2 %all-to-all-start = ((f32[512,1,128]{2,1,0:T(1,128)}), f32[512,1,128]{2,1,0:T(1,128)S(1)}, u32[]{:S(2)}, u32[]{:S(2)}) async-start(f32[512,1,128]{2,1,0:T(1,128)} %bitcast.1), calls=%async_computation | async-start | bytes 524288 | tf_op jit(solution)/shard_map/all_to_all | solution.py:179
  26.0 0.0 copy-start.8
  26.1 2.0 %shard_map.83 = f32[32,8,384]{2,1,0:T(8,128)} custom-call(f32[16,32,512]{2,1,0:T(8,128)} %k_ref.1), custom_call_target="tpu_custom_call" | custom-call | bytes 786432 | tf_op jit(solution)/shard_map/pallas_call | solution.py:168
  28.0 0.0 copy-start.5
  28.0 0.0 copy-start.6
  28.0 0.0 copy-start.7
  28.0 15.1 %all-to-all-done = f32[512,1,128]{2,1,0:T(1,128)S(1)} async-done(((f32[512,1,128]{2,1,0:T(1,128)}), f32[512,1,128]{2,1,0:T(1,128)S(1)}, u32[]{:S(2)}, u32[]{:S(2)}) %all-to-all-start) | async-done | bytes 262176 | tf_op jit(solution)/shard_map/all_to_all | solution.py:179
  43.1 19.5 %all_to_all.27.k_ref = f32[32,8,384]{2,1,0:T(8,128)S(1)} all-to-all(f32[32,8,384]{2,1,0:T(8,128)} %shard_map.83), channel_id=1, replica_groups=mesh['grp'=2,'row'=16,'col'=16] {'grp','row'}, dimensions={0} | all-to-all | bytes 786432 | tf_op jit(solution)/shard_map/all_to_all | solution.py:176
  62.7 0.0 copy-done.8
  62.7 0.0 copy-done.5
  62.7 0.0 copy-done.6
  62.7 0.0 copy-done.7
  62.7 3.1 %shard_map.84 = f32[512,128]{1,0:T(8,128)S(1)} custom-call(f32[512,128]{1,0:T(8,128)S(1)} %bitcast.9, f32[32,8,384]{2,1,0:T(8,128)S(1)} %all_to_all.27.k_ref, bf16[512,256]{1,0:T(8,128)(2,1)S(1)} %copy-done.5, bf16[512,256]{1,0:T(8,128)(2,1)S(1)} %copy-done.6, bf16[256,512]{1,0:T(8,128)(2,1)S(1)} %copy-done.7, bf16[256,512]{1,0:T(8,128)(2,1)S(1)} %copy-done.8), custom_call_target="tpu_custom_call" | custom-call | flops 1200000000 | bytes 1966080 | tf_op jit(solution)/shard_map/pallas_call | solution.py:143
  65.8 0.0 copy-start.1
  65.8 0.0 copy-start.3
  65.8 26.2 %all_to_all.28 = f32[512,1,128]{2,1,0:T(1,128)S(1)} all-to-all(f32[512,1,128]{2,1,0:T(1,128)S(1)} %bitcast.10), channel_id=1, replica_groups=mesh['grp'=2,'row'=16,'col'=16] {'col','grp','row'}, dimensions={0} | all-to-all | bytes 524288 | tf_op jit(solution)/shard_map/all_to_all | solution.py:187
  92.0 0.0 copy-done.1
  92.0 0.0 copy-done.3
  92.0 1.0 %shard_map.85 = f32[8,16,256]{2,1,0:T(8,128)} custom-call(f32[512,128]{1,0:T(8,128)S(1)} %bitcast.8, bf16[512,256]{1,0:T(8,128)(2,1)S(1)} %copy-done.1, bf16[512,256]{1,0:T(8,128)(2,1)S(1)} %copy-done.3), custom_call_target="tpu_custom_call" | custom-call | flops 100663296 | bytes 917504 | tf_op jit(solution)/shard_map/pallas_call | solution.py:143
Async XLA Ops:
  0.0 0.9 %copy-start = (bf16[512,256]{1,0:T(8,128)(2,1)S(1)}, bf16[512,256]{1,0:T(8,128)(2,1)}, u32[]{:S(2)}) copy-start(bf16[512,256]{1,0:T(8,128)(2,1)} %constant.12.clone.th_ref) | copy-start | bytes 786436
  1.0 0.9 %copy-start.2 = (bf16[512,256]{1,0:T(8,128)(2,1)S(1)}, bf16[512,256]{1,0:T(8,128)(2,1)}, u32[]{:S(2)}) copy-start(bf16[512,256]{1,0:T(8,128)(2,1)} %constant.13.clone.tl_ref) | copy-start | bytes 786436
  1.9 0.9 copy-start.4
  3.9 39.3 %all-to-all-start = ((f32[512,1,128]{2,1,0:T(1,128)}), f32[512,1,128]{2,1,0:T(1,128)S(1)}, u32[]{:S(2)}, u32[]{:S(2)}) async-start(f32[512,1,128]{2,1,0:T(1,128)} %bitcast.1), calls=%async_computation | async-start | bytes 524288 | tf_op jit(solution)/shard_map/all_to_all | solution.py:179
  26.0 36.6 %copy-start.8 = (bf16[256,512]{1,0:T(8,128)(2,1)S(1)}, bf16[256,512]{1,0:T(8,128)(2,1)}, u32[]{:S(2)}) copy-start(bf16[256,512]{1,0:T(8,128)(2,1)} %constant.17.clone.al_ref) | copy-start | bytes 786436
  28.0 34.6 %copy-start.5 = (bf16[512,256]{1,0:T(8,128)(2,1)S(1)}, bf16[512,256]{1,0:T(8,128)(2,1)}, u32[]{:S(2)}) copy-start(bf16[512,256]{1,0:T(8,128)(2,1)} %constant.14.clone.bh_ref) | copy-start | bytes 786436
  28.0 34.6 %copy-start.6 = (bf16[512,256]{1,0:T(8,128)(2,1)S(1)}, bf16[512,256]{1,0:T(8,128)(2,1)}, u32[]{:S(2)}) copy-start(bf16[512,256]{1,0:T(8,128)(2,1)} %constant.15.clone.bl_ref) | copy-start | bytes 786436
  28.0 34.6 %copy-start.7 = (bf16[256,512]{1,0:T(8,128)(2,1)S(1)}, bf16[256,512]{1,0:T(8,128)(2,1)}, u32[]{:S(2)}) copy-start(bf16[256,512]{1,0:T(8,128)(2,1)} %constant.16.clone.ah_ref) | copy-start | bytes 786436
  65.8 26.2 %copy-start.1 = (bf16[512,256]{1,0:T(8,128)(2,1)S(1)}, bf16[512,256]{1,0:T(8,128)(2,1)}, u32[]{:S(2)}) copy-start(bf16[512,256]{1,0:T(8,128)(2,1)} %constant.12.clone.th_ref) | copy-start | bytes 786436
  65.8 26.2 %copy-start.3 = (bf16[512,256]{1,0:T(8,128)(2,1)S(1)}, bf16[512,256]{1,0:T(8,128)(2,1)}, u32[]{:S(2)}) copy-start(bf16[512,256]{1,0:T(8,128)(2,1)} %constant.13.clone.tl_ref) | copy-start | bytes 786436
where the time goes:
time: 93.3 us; the launch traced here: 93 us
  blocking collectives  45.7 us (49%)
  starting transfers between devices  22.2 us (24%)
  waiting for transfers between devices  15.1 us (16%)
  Pallas kernels  7.12 us (8%)
  local copies, waits for them, and re-layouts  2.83 us (3%)
    all_to_all x1, blocking collectives, body(): got = lax.all_to_all(back, ALL, split_axis=0, concat_axis=0, tiled=True)  26.2 us
    all_to_all x1, starting transfers between devices, body(): got = lax.all_to_all(sent, ALL, split_axis=0, concat_axis=0, tiled=True)  22.2 us
    all_to_all x1, blocking collectives, body(): kernel = lax.all_to_all(picked, GA, split_axis=0, concat_axis=0, tiled=True)  19.5 us
    all_to_all x1, waiting for transfers between devices, body(): got = lax.all_to_all(sent, ALL, split_axis=0, concat_axis=0, tiled=True)  15.1 us
    pallas_call x3, Pallas kernels, call(): pl.pallas_call(kernel, out_shape=jax.ShapeDtypeStruct(shape, jnp.float32)...  5.14 us
    unnamed x18, local copies, waits for them, and re-layouts  2.83 us
    pallas_call x1, Pallas kernels, body(): pl.pallas_call(functools.partial(pick_kernel, blocks_a=blocks_a, half=cel...  1.98 us
  transfers between devices with their start and end apart: 1, of which 1 were waited for; matrix products, arithmetic and copies ran while one was open for 0% of the time, Pallas kernels for 2%

commit v1 on v0

v1 whole, which is shorter than its diff:
```python
import functools

import jax
import jax.numpy as jnp
import ml_dtypes
import numpy as np
from jax import lax
from jax.experimental import pallas as pl
from jax.experimental.pallas import tpu as pltpu
from jax.sharding import PartitionSpec as P


GA = ("grp", "row")
ALL = ("col", "grp", "row")
NN = (((1,), (0,)), ((), ()))
NT = (((1,), (1,)), ((), ()))
VMEM = pl.BlockSpec(memory_space=pltpu.VMEM)


def modes(freqs_c, freqs_s, cells, length):
    centre = np.arange(cells) - (cells - 1) / 2.0
    angle = 2.0 * np.pi / length
    return np.concatenate(
        [np.cos(angle * np.outer(freqs_c, centre)), np.sin(angle * np.outer(freqs_s, centre))], 0
    )


def halves(table):
    table = np.asarray(table, np.float32)
    hi = table.astype(ml_dtypes.bfloat16)
    lo = (table - hi.astype(np.float32)).astype(ml_dtypes.bfloat16)
    return jnp.asarray(np.stack([hi, lo]))


def split(x):
    hi = x.astype(jnp.bfloat16)
    return hi, (x - hi.astype(jnp.float32)).astype(jnp.bfloat16)


def dot3(left, right, dims):
    one = functools.partial(lax.dot_general, dimension_numbers=dims, preferred_element_type=jnp.float32)
    return one(left[0], right[0]) + (one(left[0], right[1]) + one(left[1], right[0]))


def exchange_blocks(v, block):
    count, lanes = len(v), v[0].shape[1]
    lane_block = lax.broadcasted_iota(jnp.int32, v[0].shape, 1) // block
    step = 1
    while step < count:
        odd = (lane_block & step) != 0
        w = list(v)
        for n in range(count):
            if n & step == 0:
                low, high = v[n], v[n + step]
                w[n] = jnp.where(odd, pltpu.roll(high, step * block, 1), low)
                w[n + step] = jnp.where(odd, high, pltpu.roll(low, lanes - step * block, 1))
        v = w
        step *= 2
    return v


def forward_z(d_hbm, t_hbm, out_ref, d_ref, t_ref, sems):
    copies = [
        pltpu.make_async_copy(t_hbm, t_ref, sems.at[0]),
        pltpu.make_async_copy(d_hbm, d_ref, sems.at[1]),
    ]
    for copy in copies:
        copy.start()
    for copy in copies:
        copy.wait()
    d = d_ref[...]
    d = d.reshape(d.shape[0] * d.shape[1], d.shape[2])
    out_ref[...] = dot3((t_ref[0], t_ref[1]), split(d), NT)


def pick_kernel(k_ref, out_ref, *, blocks_a, half):
    index = lax.axis_index("grp") * lax.axis_size("row") + lax.axis_index("row")
    first = jnp.where(index >= blocks_a // 2, 1, 0)
    rows, tiles = half // blocks_a, half // 128
    per = k_ref.shape[1]
    edge = k_ref[0]
    lane = lax.broadcasted_iota(jnp.int32, (per, 128), 1)
    last = pltpu.roll(edge[:, half:], rows, 1)
    for s in range(rows):
        row = k_ref[first + s]
        for h in range(tiles):
            t = s * tiles + h
            out_ref[t * per : (t + 1) * per, :] = row[:, h * 128 : (h + 1) * 128]
        column = row[:, half:]
        last = jnp.where(lane == s, pltpu.roll(column, s, 1) if s else column, last)
    for h in range(tiles):
        t = rows * tiles + h
        out_ref[t * per : (t + 1) * per, :] = edge[:, h * 128 : (h + 1) * 128]
    t = (rows + 1) * tiles
    out_ref[t * per : (t + 1) * per, :] = last


def pack(r_ref, k_ref, out_ref, *, blocks_a, blocks_b, slab_x, slab_y):
    total = out_ref.shape[0] // blocks_a
    for h in range(blocks_b // slab_x):
        first = h * slab_x * blocks_a
        v = [r_ref[first + n * blocks_a : first + (n + 1) * blocks_a, :] for n in range(slab_x)]
        v = exchange_blocks(v, slab_y)
        for n in range(slab_x):
            out_ref[pl.ds(h * slab_x + n, blocks_a, stride=total), :] = v[n]
    for t in range(blocks_b, total):
        n = t - blocks_b
        out_ref[pl.ds(t, blocks_a, stride=total), :] = k_ref[n * blocks_a : (n + 1) * blocks_a, :]


def convolve(r_ref, b_ref, a_ref, out_ref, *, blocks_a, blocks_b, slab_x, slab_y):
    half = blocks_b * slab_y
    rows, tiles = half // blocks_a, half // 128
    total = r_ref.shape[0] // blocks_a
    per = slab_x

    def take(t):
        return r_ref[pl.ds(t, blocks_a, stride=total), :]

    r = jnp.concatenate(
        [jnp.concatenate([take(h * per + n) for n in range(per)], 0) for h in range(blocks_b // per)], 1
    )
    tb = (b_ref[0], b_ref[1])
    ta = (a_ref[0], a_ref[1])
    p = dot3(tb, split(r), NT)
    q = dot3(split(p), ta, NN)
    main = jnp.concatenate(
        [
            jnp.concatenate([take(blocks_b + s * tiles + h) for s in range(rows)], 0)
            for h in range(tiles)
        ],
        1,
    )
    tail = take(blocks_b + (rows + 1) * tiles)
    column = jnp.concatenate([tail[:, s : s + 1] for s in range(rows)], 0)
    edge = blocks_a // 2 * total + blocks_b + rows * tiles
    row = jnp.concatenate([r_ref[edge + h : edge + h + 1, :] for h in range(tiles)], 1)
    corner = r_ref[edge + tiles : edge + tiles + 1, rows : rows + 1]
    row_id = lax.broadcasted_iota(jnp.int32, main.shape, 0)
    lane_id = lax.broadcasted_iota(jnp.int32, main.shape, 1)
    first_row, first_lane = row_id == 0, lane_id == 0
    scale = jnp.where(first_row, 0.5, 1.0) * jnp.where(first_lane, 0.5, 1.0) * (1.0 / (half * half))
    cc = main
    cs = jnp.where(first_lane, column, main)
    sc = jnp.where(first_row, row, main)
    ss = jnp.where(first_row, jnp.where(first_lane, corner, row), cs)
    kk = jnp.concatenate(
        [jnp.concatenate([cc * scale, cs * scale], 1), jnp.concatenate([sc * scale, ss * scale], 1)], 0
    )
    w = dot3(ta, split(q * kk), NT)
    v = dot3(split(w), tb, NN)
    for h in range(blocks_b // per):
        lanes = slice(h * per * slab_y, (h + 1) * per * slab_y)
        v_h = exchange_blocks([v[n * blocks_a : (n + 1) * blocks_a, lanes] for n in range(per)], slab_y)
        for n in range(per):
            out_ref[(h * per + n) * blocks_a : (h * per + n + 1) * blocks_a, :] = v_h[n]


def inverse_z(r_ref, t_ref, out_ref):
    r = r_ref[...]
    modes_c = r.shape[0] // 2
    row_id = lax.broadcasted_iota(jnp.int32, r.shape, 0)
    r = r * jnp.where(row_id % modes_c == 0, 0.5 / modes_c, 1.0 / modes_c)
    out = dot3(split(r.T), (t_ref[0], t_ref[1]), NN)
    out_ref[...] = out.reshape(out_ref.shape)


def call(kernel, shape, operands, flops):
    size = sum(x.size * x.dtype.itemsize for x in operands) + 4 * int(np.prod(shape))
    return pl.pallas_call(
        kernel,
        out_shape=jax.ShapeDtypeStruct(shape, jnp.float32),
        in_specs=[VMEM] * len(operands),
        out_specs=VMEM,
        compiler_params=pltpu.CompilerParams(vmem_limit_bytes=40 * 1024 * 1024),
        cost_estimate=pl.CostEstimate(flops=flops, bytes_accessed=size, transcendentals=0),
    )(*operands)


def body(density, kernel_hat):
    blocks_a = lax.axis_size(GA)
    blocks_b = lax.axis_size("col")
    slab_x, slab_y, cells = density.shape
    length = 2 * cells
    per_b, per_c = kernel_hat.shape[:2]

    tz = halves(modes(np.arange(cells), cells - np.arange(cells), cells, length))
    sub, owner = np.divmod(np.arange(cells), blocks_a)
    order_b = np.where(owner < blocks_a // 2, per_b * owner + sub, length - 1 - per_b * owner - sub)
    tb = halves(modes(order_b, np.where(order_b == 0, cells, order_b), cells, length))
    order_a = np.arange(cells)
    order_x = np.arange(cells).reshape(blocks_a, slab_x).T.reshape(-1)
    ta = halves(modes(order_a, np.where(order_a == 0, cells, order_a), cells, length)[:, order_x].T)

    rows, tiles = cells // blocks_a, cells // 128
    extra = (rows + 1) * tiles + 1
    total = blocks_b + extra
    sizes = dict(blocks_a=blocks_a, blocks_b=blocks_b, slab_x=slab_x, slab_y=slab_y)
    picked = pl.pallas_call(
        functools.partial(pick_kernel, blocks_a=blocks_a, half=cells),
        grid=(1,),
        out_shape=jax.ShapeDtypeStruct((extra * per_c, 128), jnp.float32),
        in_specs=[pl.BlockSpec((rows + 1, per_c, cells + 128), lambda i: (0, 0, 0))],
        out_specs=VMEM,
        cost_estimate=pl.CostEstimate(flops=0, bytes_accessed=8 * 32 * 8 * 384, transcendentals=0),
    )(kernel_hat)

    sent = pl.pallas_call(
        forward_z,
        out_shape=jax.ShapeDtypeStruct((length, slab_x * slab_y), jnp.float32),
        in_specs=[pl.BlockSpec(memory_space=pltpu.HBM)] * 2,
        out_specs=VMEM,
        scratch_shapes=[
            pltpu.VMEM(density.shape, jnp.float32),
            pltpu.VMEM(tz.shape, jnp.bfloat16),
            pltpu.SemaphoreType.DMA((2,)),
        ],
        cost_estimate=pl.CostEstimate(flops=6 * 128 * 256 * 512, bytes_accessed=2**20, transcendentals=0),
    )(density, tz)
    got = lax.all_to_all(sent, "col", split_axis=0, concat_axis=0, tiled=True)
    packed = call(functools.partial(pack, **sizes), (blocks_a * total, 128), (got, picked), 0)
    got = lax.all_to_all(packed.reshape(blocks_a, 1, total * 128), GA, split_axis=0, concat_axis=0, tiled=True)
    back = call(
        functools.partial(convolve, **sizes),
        (length, slab_x * slab_y),
        (got.reshape(blocks_a * total, 128), tb, ta),
        6 * 200 * 10**6,
    )
    got = lax.all_to_all(back, ALL, split_axis=0, concat_axis=0, tiled=True)
    return call(inverse_z, density.shape, (got, tz), 6 * 128 * 256 * 512)


def solution(mesh):
    return jax.shard_map(
        body,
        mesh=mesh,
        in_specs=(P(GA, "col", None), P(GA, "col", None)),
        out_specs=P(GA, "col", None),
        check_vma=False,
    )
```

time: 93.3 us -> 85.7 us (0.919)
  blocking collectives: 45.7 us -> 57.3 us
  starting transfers between devices: 22.2 us -> 11.9 us
  waiting for transfers between devices: 15.1 us -> 6.9 us
  local copies, waits for them, and re-layouts: 2.83 us -> 0.99 us
  Pallas kernels: 7.12 us -> 8.17 us
    all_to_all x1, blocking collectives: 19.5 us -> 30.5 us  [body(): lax.all_to_all(packed.reshape(blocks_a, 1, total * 128), GA, split_axis=0...]
    all_to_all x1, starting transfers between devices: 22.2 us -> 11.9 us  [body(): got = lax.all_to_all(sent, 'col', split_axis=0, concat_axis=0, tiled=True)]
    all_to_all x1, waiting for transfers between devices: 15.1 us -> 6.9 us  [body(): got = lax.all_to_all(sent, 'col', split_axis=0, concat_axis=0, tiled=True)]
    pallas_call x0 -> x1, Pallas kernels: none -> 2.16 us  [body(): pl.pallas_call(forward_z, out_shape=jax.ShapeDtypeStruct((length, slab_x...]
    unnamed x18 -> x8, local copies, waits for them, and re-layouts: 2.83 us -> 0.99 us
    pallas_call x3, Pallas kernels: 5.14 us -> 4.19 us  [call(): pl.pallas_call(kernel, out_shape=jax.ShapeDtypeStruct(shape, jnp.float32)...]
where the time goes in v1:
time: 85.7 us; the launch traced here: 85.3 us
  blocking collectives  57.3 us (67%)
  starting transfers between devices  11.9 us (14%)
  Pallas kernels  8.17 us (10%)
  waiting for transfers between devices  6.9 us (8%)
  local copies, waits for them, and re-layouts  0.99 us (1%)
    all_to_all x1, blocking collectives, body(): lax.all_to_all(packed.reshape(blocks_a, 1, total * 128), GA, split_axis=0...  30.5 us
    all_to_all x1, blocking collectives, body(): got = lax.all_to_all(back, ALL, split_axis=0, concat_axis=0, tiled=True)  26.8 us
    all_to_all x1, starting transfers between devices, body(): got = lax.all_to_all(sent, 'col', split_axis=0, concat_axis=0, tiled=True)  11.9 us
    all_to_all x1, waiting for transfers between devices, body(): got = lax.all_to_all(sent, 'col', split_axis=0, concat_axis=0, tiled=True)  6.9 us
    pallas_call x3, Pallas kernels, call(): pl.pallas_call(kernel, out_shape=jax.ShapeDtypeStruct(shape, jnp.float32)...  4.19 us
    pallas_call x1, Pallas kernels, body(): pl.pallas_call(forward_z, out_shape=jax.ShapeDtypeStruct((length, slab_x...  2.16 us
    pallas_call x1, Pallas kernels, body(): pl.pallas_call(functools.partial(pick_kernel, blocks_a=blocks_a, half=cel...  1.82 us
  transfers between devices with their start and end apart: 1, of which 1 were waited for; matrix products, arithmetic and copies ran while one was open for 0% of the time, Pallas kernels for 2%

profile of v1, /device:TPU:1, one launch (start us, length us, event | category | flops | bytes accessed | tf_op | source)
XLA Modules:
  0.0 85.3 jit_solution(478141323143176389)
XLA Ops:
  0.0 2.2 %shard_map.55 = f32[512,128]{1,0:T(8,128)} custom-call(f32[8,16,256]{2,1,0:T(8,128)} %d_hbm.1, bf16[2,512,256]{2,1,0:T(8,128)(2,1)} %constant.6.clone.t_hbm.t_ref), custom_call_target="tpu_custom_call" | custom-call | flops 100663296 | bytes 1048576 | tf_op jit(solution)/shard_map/pallas_call | solution.py:208
  2.2 11.9 %all-to-all-start = ((f32[16,32,128]{2,1,0:T(8,128)}), f32[16,32,128]{2,1,0:T(8,128)S(1)}, u32[]{:S(2)}, u32[]{:S(2)}) async-start(f32[16,32,128]{2,1,0:T(8,128)} %bitcast.13), calls=%async_computation | async-start | bytes 524288 | tf_op jit(solution)/shard_map/all_to_all | solution.py:220
  14.1 1.8 %shard_map.56.k_ref = f32[608,128]{1,0:T(8,128)} custom-call(f32[16,32,512]{2,1,0:T(8,128)} %k_ref.1), custom_call_target="tpu_custom_call" | custom-call | bytes 786432 | tf_op jit(solution)/shard_map/pallas_call | solution.py:199
  15.9 6.9 %all-to-all-done = f32[16,32,128]{2,1,0:T(8,128)S(1)} async-done(((f32[16,32,128]{2,1,0:T(8,128)}), f32[16,32,128]{2,1,0:T(8,128)S(1)}, u32[]{:S(2)}, u32[]{:S(2)}) %all-to-all-start) | async-done | bytes 262176 | tf_op jit(solution)/shard_map/all_to_all | solution.py:220
  22.8 0.0 copy-start.1
  22.8 1.0 %copy-done.1 = f32[608,128]{1,0:T(8,128)S(1)} copy-done((f32[608,128]{1,0:T(8,128)S(1)}, f32[608,128]{1,0:T(8,128)}, u32[]{:S(2)}) %copy-start.1) | copy-done | bytes 311320
  23.8 0.4 shard_map.57
  24.2 0.0 copy-start.2
  24.2 0.0 copy-start.3
  24.2 30.5 %all_to_all.27 = f32[32,1,4480]{2,1,0:T(1,128)S(1)} all-to-all(f32[32,1,4480]{2,1,0:T(1,128)S(1)} %bitcast.8), channel_id=1, replica_groups=mesh['grp'=2,'row'=16,'col'=16] {'grp','row'}, dimensions={0} | all-to-all | bytes 1146880 | tf_op jit(solution)/shard_map/all_to_all | solution.py:222
  54.7 0.0 copy-done.2
  54.7 0.0 copy-done.3
  54.7 2.8 %shard_map.58 = f32[512,128]{1,0:T(8,128)S(1)} custom-call(f32[1120,128]{1,0:T(8,128)S(1)} %bitcast.11, bf16[2,512,256]{2,1,0:T(8,128)(2,1)S(1)} %copy-done.3, bf16[2,256,512]{2,1,0:T(8,128)(2,1)S(1)} %copy-done.2), custom_call_target="tpu_custom_call" | custom-call | flops 1200000000 | bytes 1884160 | tf_op jit(solution)/shard_map/pallas_call | solution.py:170
  57.5 0.0 copy-start
  57.5 26.8 %all_to_all.28 = f32[512,1,128]{2,1,0:T(1,128)S(1)} all-to-all(f32[512,1,128]{2,1,0:T(1,128)S(1)} %bitcast.12), channel_id=1, replica_groups=mesh['grp'=2,'row'=16,'col'=16] {'col','grp','row'}, dimensions={0} | all-to-all | bytes 524288 | tf_op jit(solution)/shard_map/all_to_all | solution.py:229
  84.3 0.0 copy-done
  84.3 1.0 %shard_map.59 = f32[8,16,256]{2,1,0:T(8,128)} custom-call(f32[512,128]{1,0:T(8,128)S(1)} %bitcast.9, bf16[2,512,256]{2,1,0:T(8,128)(2,1)S(1)} %copy-done), custom_call_target="tpu_custom_call" | custom-call | flops 100663296 | bytes 917504 | tf_op jit(solution)/shard_map/pallas_call | solution.py:170
Async XLA Ops:
  2.2 20.6 %all-to-all-start = ((f32[16,32,128]{2,1,0:T(8,128)}), f32[16,32,128]{2,1,0:T(8,128)S(1)}, u32[]{:S(2)}, u32[]{:S(2)}) async-start(f32[16,32,128]{2,1,0:T(8,128)} %bitcast.13), calls=%async_computation | async-start | bytes 524288 | tf_op jit(solution)/shard_map/all_to_all | solution.py:220
  22.8 1.0 %copy-start.1 = (f32[608,128]{1,0:T(8,128)S(1)}, f32[608,128]{1,0:T(8,128)}, u32[]{:S(2)}) copy-start(f32[608,128]{1,0:T(8,128)} %shard_map.56.k_ref) | copy-start | bytes 933892
  24.2 30.5 %copy-start.2 = (bf16[2,256,512]{2,1,0:T(8,128)(2,1)S(1)}, bf16[2,256,512]{2,1,0:T(8,128)(2,1)}, u32[]{:S(2)}) copy-start(bf16[2,256,512]{2,1,0:T(8,128)(2,1)} %constant.8.clone.a_ref) | copy-start | bytes 1572868
  24.2 30.5 %copy-start.3 = (bf16[2,512,256]{2,1,0:T(8,128)(2,1)S(1)}, bf16[2,512,256]{2,1,0:T(8,128)(2,1)}, u32[]{:S(2)}) copy-start(bf16[2,512,256]{2,1,0:T(8,128)(2,1)} %constant.7.clone.b_ref) | copy-start | bytes 1572868
  57.5 26.8 %copy-start = (bf16[2,512,256]{2,1,0:T(8,128)(2,1)S(1)}, bf16[2,512,256]{2,1,0:T(8,128)(2,1)}, u32[]{:S(2)}) copy-start(bf16[2,512,256]{2,1,0:T(8,128)(2,1)} %constant.6.clone.t_hbm.t_ref) | copy-start | bytes 1572868

commit v2 on v1

v2 whole, which is shorter than its diff:
```python
import functools

import jax
import jax.numpy as jnp
import ml_dtypes
import numpy as np
from jax import lax
from jax.experimental import pallas as pl
from jax.experimental.pallas import tpu as pltpu
from jax.sharding import Mesh
from jax.sharding import PartitionSpec as P


GA = ("grp", "ra", "rb")
COL = ("ca", "cb")
RANKS = ("grp", "cb", "ra", "rb", "ca")
NN = (((1,), (0,)), ((), ()))
NT = (((1,), (1,)), ((), ()))
VMEM = pl.BlockSpec(memory_space=pltpu.VMEM)


def modes(freqs_c, freqs_s, cells, length):
    centre = np.arange(cells) - (cells - 1) / 2.0
    angle = 2.0 * np.pi / length
    return np.concatenate(
        [np.cos(angle * np.outer(freqs_c, centre)), np.sin(angle * np.outer(freqs_s, centre))], 0
    )


def halves(table):
    table = np.asarray(table, np.float32)
    hi = table.astype(ml_dtypes.bfloat16)
    lo = (table - hi.astype(np.float32)).astype(ml_dtypes.bfloat16)
    return jnp.asarray(np.stack([hi, lo]))


def split(x):
    hi = x.astype(jnp.bfloat16)
    return hi, (x - hi.astype(jnp.float32)).astype(jnp.bfloat16)


def dot3(left, right, dims):
    one = functools.partial(lax.dot_general, dimension_numbers=dims, preferred_element_type=jnp.float32)
    return one(left[0], right[0]) + (one(left[0], right[1]) + one(left[1], right[0]))


def exchange_blocks(v, block):
    count, lanes = len(v), v[0].shape[1]
    lane_block = lax.broadcasted_iota(jnp.int32, v[0].shape, 1) // block
    step = 1
    while step < count:
        odd = (lane_block & step) != 0
        w = list(v)
        for n in range(count):
            if n & step == 0:
                low, high = v[n], v[n + step]
                w[n] = jnp.where(odd, pltpu.roll(high, step * block, 1), low)
                w[n + step] = jnp.where(odd, high, pltpu.roll(low, lanes - step * block, 1))
        v = w
        step *= 2
    return v


def forward_z(d_hbm, t_hbm, out_ref, d_ref, t_ref, sems):
    copies = [
        pltpu.make_async_copy(t_hbm, t_ref, sems.at[0]),
        pltpu.make_async_copy(d_hbm, d_ref, sems.at[1]),
    ]
    for copy in copies:
        copy.start()
    for copy in copies:
        copy.wait()
    d = d_ref[...]
    d = d.reshape(d.shape[0] * d.shape[1], d.shape[2])
    out_ref[...] = dot3((t_ref[0], t_ref[1]), split(d), NT)


def pack(r_ref, k_ref, out_ref, *, blocks_a, blocks_b, slab_x, slab_y):
    half = blocks_b * slab_y
    rows, tiles = half // blocks_a, half // 128
    total = out_ref.shape[0] // blocks_a

    def put(t, value):
        out_ref[pl.ds(t, blocks_a, stride=total), :] = value

    for h in range(blocks_b // slab_x):
        first = h * slab_x * blocks_a
        v = [r_ref[first + n * blocks_a : first + (n + 1) * blocks_a, :] for n in range(slab_x)]
        v = exchange_blocks(v, slab_y)
        for n in range(slab_x):
            put(h * slab_x + n, v[n])
    first = lax.axis_index("grp")
    lane = lax.broadcasted_iota(jnp.int32, (blocks_a, 128), 1)
    last = pltpu.roll(k_ref[0, :, half : half + 128], rows, 1)
    for s in range(rows):
        for h in range(tiles):
            put(blocks_b + s * tiles + h, k_ref[first + s, :, h * 128 : (h + 1) * 128])
        column = k_ref[first + s, :, half : half + 128]
        last = jnp.where(lane == s, pltpu.roll(column, s, 1) if s else column, last)
    for h in range(tiles):
        put(blocks_b + rows * tiles + h, k_ref[0, :, h * 128 : (h + 1) * 128])
    put(blocks_b + (rows + 1) * tiles, last)


def convolve(r_ref, y_ref, x_ref, y_back_ref, x_back_ref, out_ref, *, blocks_a, blocks_b, slab_x, slab_y, runs):
    half = blocks_b * slab_y
    rows, tiles = half // blocks_a, half // 128
    total = r_ref.shape[0] // blocks_a
    per = slab_x

    def take(t):
        return r_ref[pl.ds(t, blocks_a, stride=total), :]

    r = jnp.concatenate(
        [jnp.concatenate([take(h * per + n) for n in range(per)], 0) for h in range(blocks_b // per)], 1
    )
    main = jnp.concatenate(
        [
            jnp.concatenate([take(blocks_b + s * tiles + h) for s in range(rows)], 0).T
            for h in range(tiles)
        ],
        0,
    )
    tail = take(blocks_b + (rows + 1) * tiles).T
    line = jnp.concatenate([tail[s : s + 1] for s in range(rows)], 1)
    edge = blocks_a // 2 * total + blocks_b + rows * tiles
    column = jnp.concatenate(
        [jnp.broadcast_to(r_ref[edge + h : edge + h + 1, :], (8, 128)).T[:, :1] for h in range(tiles)], 0
    )
    corner = r_ref[edge + tiles : edge + tiles + 1, rows : rows + 1]
    first_row = lax.broadcasted_iota(jnp.int32, main.shape, 0) == 0
    first_lane = lax.broadcasted_iota(jnp.int32, main.shape, 1) == 0
    lined = jnp.where(first_row, line, main)
    with_column = jnp.where(first_row, corner, column)
    kernels = (
        jnp.concatenate([main, jnp.where(first_lane, column, main)], 1),
        jnp.concatenate([lined, jnp.where(first_lane, with_column, lined)], 1),
    )
    p = split(dot3(split(r), (y_ref[0], y_ref[1]), NN))
    y_back = (y_back_ref[0], y_back_ref[1])
    u = []
    for part in range(2):
        at = slice(part * half, (part + 1) * half)
        q = dot3((x_ref[0, at], x_ref[1, at]), p, NN) * kernels[part]
        u.append(dot3(split(q), y_back, NN))
    v = dot3((x_back_ref[0], x_back_ref[1]), split(jnp.concatenate(u, 0)), NN)
    for h in range(blocks_b // per):
        lanes = slice(h * per * slab_y, (h + 1) * per * slab_y)
        v_h = exchange_blocks([v[n * blocks_a : (n + 1) * blocks_a, lanes] for n in range(per)], slab_y)
        for n in range(per):
            done = 0
            for start, step, count in runs[h * per + n]:
                out_ref[pl.ds(start, count, stride=step), :] = v_h[n][done : done + count]
                done += count


def inverse_z(r_ref, t_ref, out_ref):
    out = dot3(split(r_ref[...].T), (t_ref[0], t_ref[1]), NN)
    out_ref[...] = out.reshape(out_ref.shape)


def strided(values):
    runs, at = [], 0
    while at < len(values):
        step = values[at + 1] - values[at] if at + 1 < len(values) else 1
        count = 1
        while at + count < len(values) and values[at + count] - values[at + count - 1] == step:
            count += 1
        runs.append((int(values[at]), int(step), count))
        at += count
    return tuple(runs)


def call(kernel, shape, operands, flops):
    size = sum(x.size * x.dtype.itemsize for x in operands) + 4 * int(np.prod(shape))
    return pl.pallas_call(
        kernel,
        out_shape=jax.ShapeDtypeStruct(shape, jnp.float32),
        in_specs=[VMEM] * len(operands),
        out_specs=VMEM,
        compiler_params=pltpu.CompilerParams(vmem_limit_bytes=40 * 1024 * 1024),
        cost_estimate=pl.CostEstimate(flops=flops, bytes_accessed=size, transcendentals=0),
    )(*operands)


def body(density, kernel_hat):
    blocks_a = lax.axis_size(GA)
    blocks_b = lax.axis_size(COL)
    slab_x, slab_y, cells = density.shape
    length = 2 * cells
    per_b, per_c = kernel_hat.shape[:2]
    weights = np.full((2, cells), 2.0 / length)
    weights[:, 0] = 1.0 / length
    weights = weights.reshape(length, 1)

    sizes = {name: lax.axis_size(name) for name in RANKS}
    where = dict(zip(RANKS, np.indices(tuple(sizes.values())).reshape(len(RANKS), -1)))
    index_a = np.ravel_multi_index([where[n] for n in GA], [sizes[n] for n in GA])
    index_b = np.ravel_multi_index([where[n] for n in COL], [sizes[n] for n in COL])
    ranks = np.empty((blocks_a, blocks_b), np.int64)
    ranks[index_a, index_b] = np.arange(len(index_a))
    order_blocks = np.argsort(ranks[:, 0])
    runs = tuple(strided(ranks[order_blocks, n]) for n in range(blocks_b))

    modes_z = modes(np.arange(cells), cells - np.arange(cells), cells, length)
    tz = halves(modes_z)
    tz_back = halves((weights * modes_z)[per_c * index_b + index_a])
    sub, owner = np.divmod(np.arange(cells), blocks_a)
    order_b = np.where(owner < blocks_a // 2, per_b * owner + sub, length - 1 - per_b * owner - sub)
    modes_y = modes(order_b, np.where(order_b == 0, cells, order_b), cells, length)
    ty, ty_back = halves(modes_y.T), halves(weights * modes_y)
    order_a = np.arange(cells)
    modes_x = modes(order_a, np.where(order_a == 0, cells, order_a), cells, length)
    order_x = np.arange(cells).reshape(blocks_a, slab_x).T
    tx = halves(modes_x[:, order_x.reshape(-1)])
    tx_back = halves((weights * modes_x)[:, order_x[:, order_blocks].reshape(-1)].T)

    rows, tiles = cells // blocks_a, cells // 128
    total = blocks_b + (rows + 1) * tiles + 1
    places = dict(blocks_a=blocks_a, blocks_b=blocks_b, slab_x=slab_x, slab_y=slab_y)

    sent = pl.pallas_call(
        forward_z,
        out_shape=jax.ShapeDtypeStruct((length, slab_x * slab_y), jnp.float32),
        in_specs=[pl.BlockSpec(memory_space=pltpu.HBM)] * 2,
        out_specs=VMEM,
        scratch_shapes=[
            pltpu.VMEM(density.shape, jnp.float32),
            pltpu.VMEM(tz.shape, jnp.bfloat16),
            pltpu.SemaphoreType.DMA((2,)),
        ],
        compiler_params=pltpu.CompilerParams(vmem_limit_bytes=8 * 1024 * 1024),
        cost_estimate=pl.CostEstimate(flops=6 * 128 * 256 * 512, bytes_accessed=2**20, transcendentals=0),
    )(density, tz)
    got = lax.all_to_all(sent, COL, split_axis=0, concat_axis=0, tiled=True)
    packed = call(functools.partial(pack, **places), (blocks_a * total, 128), (got, kernel_hat), 0)
    got = lax.all_to_all(packed.reshape(blocks_a, 1, total * 128), GA, split_axis=0, concat_axis=0, tiled=True)
    back = call(
        functools.partial(convolve, runs=runs, **places),
        (length, slab_x * slab_y),
        (got.reshape(blocks_a * total, 128), ty, tx, ty_back, tx_back),
        6 * 200 * 10**6,
    )
    got = lax.all_to_all(back, RANKS, split_axis=0, concat_axis=0, tiled=True)
    return call(inverse_z, density.shape, (got, tz_back), 6 * 128 * 256 * 512)


def solution(mesh):
    devices = mesh.devices
    grp, row, col = devices.shape
    parts = Mesh(devices.reshape(grp, row // 2, 2, 2, col // 2), ("grp", "ra", "rb", "ca", "cb"))
    return jax.shard_map(
        body,
        mesh=parts,
        in_specs=(P(GA, COL, None), P(GA, COL, None)),
        out_specs=P(GA, COL, None),
        check_vma=False,
    )
```

time: 85.7 us -> 84.2 us (0.982)
  blocking collectives: 57.3 us -> 77.7 us
  starting transfers between devices: 11.9 us -> 0 us
  waiting for transfers between devices: 6.9 us -> 0 us
  Pallas kernels: 8.17 us -> 4.28 us
  local copies, waits for them, and re-layouts: 0.99 us -> 1.98 us
    all_to_all x1 -> x2, blocking collectives: 26.8 us -> 47.1 us  [the longest x1 26.7 us: body(): got = lax.all_to_all(back, RANKS, split_axis=0, concat_axis=0, tiled=True)]
    all_to_all x1 -> x0, starting transfers between devices: 11.9 us -> none  [body(): got = lax.all_to_all(sent, 'col', split_axis=0, concat_axis=0, tiled=True)]
    all_to_all x1 -> x0, waiting for transfers between devices: 6.9 us -> none  [body(): got = lax.all_to_all(sent, 'col', split_axis=0, concat_axis=0, tiled=True)]
    pallas_call x1 -> x0, Pallas kernels: 1.82 us -> none  [body(): pl.pallas_call(functools.partial(pick_kernel, blocks_a=blocks_a, half=cel...]
    pallas_call x1, Pallas kernels: 2.16 us -> 0.59 us  [body(): pl.pallas_call(forward_z, out_shape=jax.ShapeDtypeStruct((length, slab_x...]
    unnamed x8 -> x16, local copies, waits for them, and re-layouts: 0.99 us -> 1.98 us
  transfers between devices with their start and end apart: 1 -> 0, of which waited for: 1 -> 0; matrix products, arithmetic and copies ran while one was open for 0% -> 0% of each run, Pallas kernels for 2% -> 0%
where the time goes in v2:
time: 84.2 us; the launch traced here: 84 us
  blocking collectives  77.7 us (92%)
  Pallas kernels  4.28 us (5%)
  local copies, waits for them, and re-layouts  1.98 us (2%)
    all_to_all x1, blocking collectives, body(): lax.all_to_all(packed.reshape(blocks_a, 1, total * 128), GA, split_axis=0...  30.5 us
    all_to_all x1, blocking collectives, body(): got = lax.all_to_all(back, RANKS, split_axis=0, concat_axis=0, tiled=True)  26.7 us
    all_to_all x1, blocking collectives, body(): got = lax.all_to_all(sent, COL, split_axis=0, concat_axis=0, tiled=True)  20.4 us
    pallas_call x3, Pallas kernels, call(): pl.pallas_call(kernel, out_shape=jax.ShapeDtypeStruct(shape, jnp.float32)...  3.69 us
    unnamed x16, local copies, waits for them, and re-layouts  1.98 us

profile of v2, /device:TPU:1, one launch (start us, length us, event | category | flops | bytes accessed | tf_op | source)
XLA Modules:
  0.0 84.0 jit_solution(9651068576952394853)
XLA Ops:
  0.0 0.0 copy-start.2
  0.0 1.0 %copy-done.2 = bf16[2,512,256]{2,1,0:T(8,128)(2,1)S(1)} copy-done((bf16[2,512,256]{2,1,0:T(8,128)(2,1)S(1)}, bf16[2,512,256]{2,1,0:T(8,128)(2,1)}, u32[]{:S(2)}) %copy-start.2) | copy-done | bytes 524312
  1.0 0.0 copy-start.3
  1.0 0.9 %copy-done.3 = f32[8,16,256]{2,1,0:T(8,128)S(1)} copy-done((f32[8,16,256]{2,1,0:T(8,128)S(1)}, f32[8,16,256]{2,1,0:T(8,128)}, u32[]{:S(2)}) %copy-start.3) | copy-done | bytes 131096
  1.9 0.0 copy-start
  1.9 0.6 shard_map.82
  2.5 20.4 %all_to_all.27 = f32[16,32,128]{2,1,0:T(8,128)S(1)} all-to-all(f32[16,32,128]{2,1,0:T(8,128)S(1)} %bitcast.10), channel_id=1, replica_groups=mesh['grp'=2,'ra'=8,'rb'=2,'ca'=2,'cb'=8] {'ca','cb'}, dimensions={0} | all-to-all | bytes 524288 | tf_op jit(solution)/shard_map/all_to_all | solution.py:235
  23.0 0.0 copy-done
  23.0 0.0 copy-start.6
  23.0 0.0 copy-start.7
  23.0 0.4 shard_map.83
  23.4 0.0 copy-start.4
  23.4 0.0 copy-start.5
  23.4 30.5 %all_to_all.28 = f32[32,1,4480]{2,1,0:T(1,128)S(1)} all-to-all(f32[32,1,4480]{2,1,0:T(1,128)S(1)} %bitcast.8), channel_id=1, replica_groups=mesh['grp'=2,'ra'=8,'rb'=2,'ca'=2,'cb'=8] {'grp','ra','rb'}, dimensions={0} | all-to-all | bytes 1146880 | tf_op jit(solution)/shard_map/all_to_all | solution.py:237
  54.0 0.0 copy-done.6
  54.0 0.0 copy-done.7
  54.0 0.0 copy-done.4
  54.0 0.0 copy-done.5
  54.0 2.3 %shard_map.84 = f32[512,128]{1,0:T(8,128)S(1)} custom-call(f32[1120,128]{1,0:T(8,128)S(1)} %bitcast.12, bf16[2,256,512]{2,1,0:T(8,128)(2,1)S(1)} %copy-done.7, bf16[2,512,256]{2,1,0:T(8,128)(2,1)S(1)} %copy-done.5, bf16[2,512,256]{2,1,0:T(8,128)(2,1)S(1)} %copy-done.6, bf16[2,256,512]{2,1,0:T(8,128)(2,1)S(1)} %copy-done.4), custom_call_target="tpu_custom_call" | custom-call | flops 1200000000 | bytes 2932736 | tf_op jit(solution)/shard_map/pallas_call | solution.py:176
  56.3 0.0 copy-start.1
  56.3 26.7 %all_to_all.29 = f32[512,1,128]{2,1,0:T(1,128)S(1)} all-to-all(f32[512,1,128]{2,1,0:T(1,128)S(1)} %bitcast.13), channel_id=1, replica_groups=mesh['grp'=2,'ra'=8,'rb'=2,'ca'=2,'cb'=8] {'grp','cb','ra','rb','ca'}, dimensions={0} | all-to-all | bytes 524288 | tf_op jit(solution)/shard_map/all_to_all | solution.py:244
  83.0 0.0 copy-done.1
  83.0 1.0 %shard_map.85 = f32[8,16,256]{2,1,0:T(8,128)} custom-call(f32[512,128]{1,0:T(8,128)S(1)} %bitcast.9, bf16[2,512,256]{2,1,0:T(8,128)(2,1)S(1)} %copy-done.1), custom_call_target="tpu_custom_call" | custom-call | flops 100663296 | bytes 917504 | tf_op jit(solution)/shard_map/pallas_call | solution.py:176
Async XLA Ops:
  0.0 1.0 %copy-start.2 = (bf16[2,512,256]{2,1,0:T(8,128)(2,1)S(1)}, bf16[2,512,256]{2,1,0:T(8,128)(2,1)}, u32[]{:S(2)}) copy-start(bf16[2,512,256]{2,1,0:T(8,128)(2,1)} %constant.12.clone.t_hbm) | copy-start | bytes 1572868
  1.0 0.9 %copy-start.3 = (f32[8,16,256]{2,1,0:T(8,128)S(1)}, f32[8,16,256]{2,1,0:T(8,128)}, u32[]{:S(2)}) copy-start(f32[8,16,256]{2,1,0:T(8,128)} %d_hbm.1) | copy-start | bytes 393220
  1.9 21.0 %copy-start = (f32[16,32,512]{2,1,0:T(8,128)S(1)}, f32[16,32,512]{2,1,0:T(8,128)}, u32[]{:S(2)}) copy-start(f32[16,32,512]{2,1,0:T(8,128)} %k_ref.1) | copy-start | bytes 3145732
  23.0 31.0 %copy-start.6 = (bf16[2,512,256]{2,1,0:T(8,128)(2,1)S(1)}, bf16[2,512,256]{2,1,0:T(8,128)(2,1)}, u32[]{:S(2)}) copy-start(bf16[2,512,256]{2,1,0:T(8,128)(2,1)} %constant.15.clone.y_back_ref) | copy-start | bytes 1572868
  23.0 31.0 %copy-start.7 = (bf16[2,256,512]{2,1,0:T(8,128)(2,1)S(1)}, bf16[2,256,512]{2,1,0:T(8,128)(2,1)}, u32[]{:S(2)}) copy-start(bf16[2,256,512]{2,1,0:T(8,128)(2,1)} %constant.14.clone.y_ref) | copy-start | bytes 1572868
  23.4 30.5 %copy-start.4 = (bf16[2,256,512]{2,1,0:T(8,128)(2,1)S(1)}, bf16[2,256,512]{2,1,0:T(8,128)(2,1)}, u32[]{:S(2)}) copy-start(bf16[2,256,512]{2,1,0:T(8,128)(2,1)} %constant.17.clone.x_back_ref) | copy-start | bytes 1572868
  23.4 30.5 %copy-start.5 = (bf16[2,512,256]{2,1,0:T(8,128)(2,1)S(1)}, bf16[2,512,256]{2,1,0:T(8,128)(2,1)}, u32[]{:S(2)}) copy-start(bf16[2,512,256]{2,1,0:T(8,128)(2,1)} %constant.16.clone.x_ref) | copy-start | bytes 1572868
  56.3 26.7 %copy-start.1 = (bf16[2,512,256]{2,1,0:T(8,128)(2,1)S(1)}, bf16[2,512,256]{2,1,0:T(8,128)(2,1)}, u32[]{:S(2)}) copy-start(bf16[2,512,256]{2,1,0:T(8,128)(2,1)} %constant.13.clone.t_ref) | copy-start | bytes 1572868

commit v3 on v2

--- a/solution.py
+++ b/solution.py
@@ -1,4 +1,5 @@
 import functools
+import math
 
 import jax
 import jax.numpy as jnp
@@ -61,18 +62,27 @@
     return v
 
 
-def forward_z(d_hbm, t_hbm, out_ref, d_ref, t_ref, sems):
-    copies = [
-        pltpu.make_async_copy(t_hbm, t_ref, sems.at[0]),
-        pltpu.make_async_copy(d_hbm, d_ref, sems.at[1]),
-    ]
-    for copy in copies:
-        copy.start()
-    for copy in copies:
-        copy.wait()
+def table_z(length, cells, step=16):
+    def pair(rows, scale):
+        n = lax.broadcasted_iota(jnp.int32, (rows, cells), 0) * scale
+        offset = 2 * lax.broadcasted_iota(jnp.int32, (rows, cells), 1) - (cells - 1)
+        turn = lax.rem(n * offset, 2 * length)
+        angle = turn.astype(jnp.float32) * (math.pi / length)
+        return jnp.cos(angle), jnp.sin(angle)
+
+    cos_u, sin_u = pair(length // step, step)
+    cos_v, sin_v = pair(step, 1)
+    blocks = []
+    for u in range(length // step):
+        c, s = cos_u[u : u + 1], sin_u[u : u + 1]
+        blocks.append(c * cos_v - s * sin_v if 2 * u * step < length else s * cos_v + c * sin_v)
+    return jnp.concatenate(blocks, 0)
+
+
+def forward_z(d_ref, out_ref):
     d = d_ref[...]
     d = d.reshape(d.shape[0] * d.shape[1], d.shape[2])
-    out_ref[...] = dot3((t_ref[0], t_ref[1]), split(d), NT)
+    out_ref[...] = dot3(split(table_z(out_ref.shape[0], d.shape[1])), split(d), NT)
 
 
 def pack(r_ref, k_ref, out_ref, *, blocks_a, blocks_b, slab_x, slab_y):
@@ -203,7 +213,6 @@
     runs = tuple(strided(ranks[order_blocks, n]) for n in range(blocks_b))
 
     modes_z = modes(np.arange(cells), cells - np.arange(cells), cells, length)
-    tz = halves(modes_z)
     tz_back = halves((weights * modes_z)[per_c * index_b + index_a])
     sub, owner = np.divmod(np.arange(cells), blocks_a)
     order_b = np.where(owner < blocks_a // 2, per_b * owner + sub, length - 1 - per_b * owner - sub)
@@ -219,19 +228,7 @@
     total = blocks_b + (rows + 1) * tiles + 1
     places = dict(blocks_a=blocks_a, blocks_b=blocks_b, slab_x=slab_x, slab_y=slab_y)
 
-    sent = pl.pallas_call(
-        forward_z,
-        out_shape=jax.ShapeDtypeStruct((length, slab_x * slab_y), jnp.float32),
-        in_specs=[pl.BlockSpec(memory_space=pltpu.HBM)] * 2,
-        out_specs=VMEM,
-        scratch_shapes=[
-            pltpu.VMEM(density.shape, jnp.float32),
-            pltpu.VMEM(tz.shape, jnp.bfloat16),
-            pltpu.SemaphoreType.DMA((2,)),
-        ],
-        compiler_params=pltpu.CompilerParams(vmem_limit_bytes=8 * 1024 * 1024),
-        cost_estimate=pl.CostEstimate(flops=6 * 128 * 256 * 512, bytes_accessed=2**20, transcendentals=0),
-    )(density, tz)
+    sent = call(forward_z, (length, slab_x * slab_y), (density,), 10**9)
     got = lax.all_to_all(sent, COL, split_axis=0, concat_axis=0, tiled=True)
     packed = call(functools.partial(pack, **places), (blocks_a * total, 128), (got, kernel_hat), 0)
     got = lax.all_to_all(packed.reshape(blocks_a, 1, total * 128), GA, split_axis=0, concat_axis=0, tiled=True)

time: 84.2 us -> 83.1 us (0.987)
  local copies, waits for them, and re-layouts: 1.98 us -> 0.94 us
    unnamed x16 -> x14, local copies, waits for them, and re-layouts: 1.98 us -> 0.94 us
    pallas_call x3 -> x4, Pallas kernels: 3.69 us -> 4.28 us  [call(): pl.pallas_call(kernel, out_shape=jax.ShapeDtypeStruct(shape, jnp.float32)...]
where the time goes in v3:
time: 83.1 us; the launch traced here: 82.9 us
  blocking collectives  77.7 us (94%)
  Pallas kernels  4.28 us (5%)
  local copies, waits for them, and re-layouts  0.94 us (1%)
    all_to_all x1, blocking collectives, body(): lax.all_to_all(packed.reshape(blocks_a, 1, total * 128), GA, split_axis=0...  30.5 us
    all_to_all x1, blocking collectives, body(): got = lax.all_to_all(back, RANKS, split_axis=0, concat_axis=0, tiled=True)  26.7 us
    all_to_all x1, blocking collectives, body(): got = lax.all_to_all(sent, COL, split_axis=0, concat_axis=0, tiled=True)  20.4 us
    pallas_call x4, Pallas kernels, call(): pl.pallas_call(kernel, out_shape=jax.ShapeDtypeStruct(shape, jnp.float32)...  4.28 us

profile of v3, /device:TPU:1, one launch (start us, length us, event | category | flops | bytes accessed | tf_op | source)
XLA Modules:
  0.0 82.9 jit_solution(4703481541467724583)
XLA Ops:
  0.0 0.0 copy-start.2
  0.0 0.9 %copy-done.2 = f32[8,16,256]{2,1,0:T(8,128)S(1)} copy-done((f32[8,16,256]{2,1,0:T(8,128)S(1)}, f32[8,16,256]{2,1,0:T(8,128)}, u32[]{:S(2)}) %copy-start.2) | copy-done | bytes 131096
  0.9 0.0 copy-start
  0.9 0.6 shard_map.73
  1.5 20.4 %all_to_all.27 = f32[16,32,128]{2,1,0:T(8,128)S(1)} all-to-all(f32[16,32,128]{2,1,0:T(8,128)S(1)} %bitcast.13), channel_id=1, replica_groups=mesh['grp'=2,'ra'=8,'rb'=2,'ca'=2,'cb'=8] {'ca','cb'}, dimensions={0} | all-to-all | bytes 524288 | tf_op jit(solution)/shard_map/all_to_all | solution.py:232
  21.9 0.0 copy-done
  21.9 0.0 copy-start.5
  21.9 0.0 copy-start.6
  21.9 0.4 shard_map.74
  22.4 0.0 copy-start.3
  22.4 0.0 copy-start.4
  22.4 30.5 %all_to_all.28 = f32[32,1,4480]{2,1,0:T(1,128)S(1)} all-to-all(f32[32,1,4480]{2,1,0:T(1,128)S(1)} %bitcast.8), channel_id=1, replica_groups=mesh['grp'=2,'ra'=8,'rb'=2,'ca'=2,'cb'=8] {'grp','ra','rb'}, dimensions={0} | all-to-all | bytes 1146880 | tf_op jit(solution)/shard_map/all_to_all | solution.py:234
  52.9 0.0 copy-done.5
  52.9 0.0 copy-done.6
  52.9 0.0 copy-done.3
  52.9 0.0 copy-done.4
  52.9 2.3 %shard_map.75 = f32[512,128]{1,0:T(8,128)S(1)} custom-call(f32[1120,128]{1,0:T(8,128)S(1)} %bitcast.11, bf16[2,256,512]{2,1,0:T(8,128)(2,1)S(1)} %copy-done.6, bf16[2,512,256]{2,1,0:T(8,128)(2,1)S(1)} %copy-done.4, bf16[2,512,256]{2,1,0:T(8,128)(2,1)S(1)} %copy-done.5, bf16[2,256,512]{2,1,0:T(8,128)(2,1)S(1)} %copy-done.3), custom_call_target="tpu_custom_call" | custom-call | flops 1200000000 | bytes 2932736 | tf_op jit(solution)/shard_map/pallas_call | solution.py:186
  55.2 0.0 copy-start.1
  55.2 26.7 %all_to_all.29 = f32[512,1,128]{2,1,0:T(1,128)S(1)} all-to-all(f32[512,1,128]{2,1,0:T(1,128)S(1)} %bitcast.12), channel_id=1, replica_groups=mesh['grp'=2,'ra'=8,'rb'=2,'ca'=2,'cb'=8] {'grp','cb','ra','rb','ca'}, dimensions={0} | all-to-all | bytes 524288 | tf_op jit(solution)/shard_map/all_to_all | solution.py:241
  81.9 0.0 copy-done.1
  81.9 1.0 %shard_map.76 = f32[8,16,256]{2,1,0:T(8,128)} custom-call(f32[512,128]{1,0:T(8,128)S(1)} %bitcast.9, bf16[2,512,256]{2,1,0:T(8,128)(2,1)S(1)} %copy-done.1), custom_call_target="tpu_custom_call" | custom-call | flops 100663296 | bytes 917504 | tf_op jit(solution)/shard_map/pallas_call | solution.py:186
Async XLA Ops:
  0.0 0.9 %copy-start.2 = (f32[8,16,256]{2,1,0:T(8,128)S(1)}, f32[8,16,256]{2,1,0:T(8,128)}, u32[]{:S(2)}) copy-start(f32[8,16,256]{2,1,0:T(8,128)} %d_ref.1) | copy-start | bytes 393220
  0.9 21.0 %copy-start = (f32[16,32,512]{2,1,0:T(8,128)S(1)}, f32[16,32,512]{2,1,0:T(8,128)}, u32[]{:S(2)}) copy-start(f32[16,32,512]{2,1,0:T(8,128)} %k_ref.1) | copy-start | bytes 3145732
  21.9 31.0 %copy-start.5 = (bf16[2,512,256]{2,1,0:T(8,128)(2,1)S(1)}, bf16[2,512,256]{2,1,0:T(8,128)(2,1)}, u32[]{:S(2)}) copy-start(bf16[2,512,256]{2,1,0:T(8,128)(2,1)} %constant.12.clone.y_back_ref) | copy-start | bytes 1572868
  21.9 31.0 %copy-start.6 = (bf16[2,256,512]{2,1,0:T(8,128)(2,1)S(1)}, bf16[2,256,512]{2,1,0:T(8,128)(2,1)}, u32[]{:S(2)}) copy-start(bf16[2,256,512]{2,1,0:T(8,128)(2,1)} %constant.11.clone.y_ref) | copy-start | bytes 1572868
  22.4 30.5 %copy-start.3 = (bf16[2,256,512]{2,1,0:T(8,128)(2,1)S(1)}, bf16[2,256,512]{2,1,0:T(8,128)(2,1)}, u32[]{:S(2)}) copy-start(bf16[2,256,512]{2,1,0:T(8,128)(2,1)} %constant.14.clone.x_back_ref) | copy-start | bytes 1572868
  22.4 30.5 %copy-start.4 = (bf16[2,512,256]{2,1,0:T(8,128)(2,1)S(1)}, bf16[2,512,256]{2,1,0:T(8,128)(2,1)}, u32[]{:S(2)}) copy-start(bf16[2,512,256]{2,1,0:T(8,128)(2,1)} %constant.13.clone.x_ref) | copy-start | bytes 1572868
  55.2 26.7 %copy-start.1 = (bf16[2,512,256]{2,1,0:T(8,128)(2,1)S(1)}, bf16[2,512,256]{2,1,0:T(8,128)(2,1)}, u32[]{:S(2)}) copy-start(bf16[2,512,256]{2,1,0:T(8,128)(2,1)} %constant.10.clone.t_ref) | copy-start | bytes 1572868

commit v4 on v3

--- a/solution.py
+++ b/solution.py
@@ -100,16 +100,20 @@
         for n in range(slab_x):
             put(h * slab_x + n, v[n])
     first = lax.axis_index("grp")
+    edge = jnp.logical_and(first == 1, lax.axis_index("ra") + lax.axis_index("rb") == 0)
     lane = lax.broadcasted_iota(jnp.int32, (blocks_a, 128), 1)
     last = pltpu.roll(k_ref[0, :, half : half + 128], rows, 1)
+    end = half - 128
     for s in range(rows):
         for h in range(tiles):
-            put(blocks_b + s * tiles + h, k_ref[first + s, :, h * 128 : (h + 1) * 128])
+            tile = k_ref[first + s, :, h * 128 : (h + 1) * 128]
+            if s == rows - 1 and h == tiles - 1:
+                tile = jnp.where(edge, k_ref[0, :, end:half], tile)
+            put(blocks_b + s * tiles + h, tile)
         column = k_ref[first + s, :, half : half + 128]
         last = jnp.where(lane == s, pltpu.roll(column, s, 1) if s else column, last)
-    for h in range(tiles):
-        put(blocks_b + rows * tiles + h, k_ref[0, :, h * 128 : (h + 1) * 128])
-    put(blocks_b + (rows + 1) * tiles, last)
+    put(blocks_b + rows * tiles, jnp.where(edge, k_ref[0, :, :128], k_ref[rows, :, end:half]))
+    put(blocks_b + rows * tiles + 1, last)
 
 
 def convolve(r_ref, y_ref, x_ref, y_back_ref, x_back_ref, out_ref, *, blocks_a, blocks_b, slab_x, slab_y, runs):
@@ -124,20 +128,26 @@
     r = jnp.concatenate(
         [jnp.concatenate([take(h * per + n) for n in range(per)], 0) for h in range(blocks_b // per)], 1
     )
+    spare, middle = blocks_b + rows * tiles, blocks_a // 2
+
+    def kernel_tile(s, h):
+        tile = take(blocks_b + s * tiles + h)
+        if s == rows - 1 and h == tiles - 1:
+            at = (middle - 1) * total + spare
+            owner = lax.broadcasted_iota(jnp.int32, tile.shape, 0)
+            tile = jnp.where(owner == middle, r_ref[at : at + 1, :], tile)
+        return tile
+
     main = jnp.concatenate(
-        [
-            jnp.concatenate([take(blocks_b + s * tiles + h) for s in range(rows)], 0).T
-            for h in range(tiles)
-        ],
-        0,
-    )
-    tail = take(blocks_b + (rows + 1) * tiles).T
+        [jnp.concatenate([kernel_tile(s, h) for s in range(rows)], 0).T for h in range(tiles)], 0
+    )
+    tail = take(spare + 1).T
     line = jnp.concatenate([tail[s : s + 1] for s in range(rows)], 1)
-    edge = blocks_a // 2 * total + blocks_b + rows * tiles
+    at = middle * total + spare
     column = jnp.concatenate(
-        [jnp.broadcast_to(r_ref[edge + h : edge + h + 1, :], (8, 128)).T[:, :1] for h in range(tiles)], 0
-    )
-    corner = r_ref[edge + tiles : edge + tiles + 1, rows : rows + 1]
+        [jnp.broadcast_to(r_ref[n : n + 1, :], (8, 128)).T[:, :1] for n in (at, at - 1)], 0
+    )
+    corner = r_ref[at + 1 : at + 2, rows : rows + 1]
     first_row = lax.broadcasted_iota(jnp.int32, main.shape, 0) == 0
     first_lane = lax.broadcasted_iota(jnp.int32, main.shape, 1) == 0
     lined = jnp.where(first_row, line, main)
@@ -225,7 +235,7 @@
     tx_back = halves((weights * modes_x)[:, order_x[:, order_blocks].reshape(-1)].T)
 
     rows, tiles = cells // blocks_a, cells // 128
-    total = blocks_b + (rows + 1) * tiles + 1
+    total = blocks_b + rows * tiles + 2
     places = dict(blocks_a=blocks_a, blocks_b=blocks_b, slab_x=slab_x, slab_y=slab_y)
 
     sent = call(forward_z, (length, slab_x * slab_y), (density,), 10**9)

time: 83.1 us -> 82.8 us (level)
  no operation moved by 1% of the time
where the time goes in v4:
time: 82.8 us; the launch traced here: 82.6 us
  blocking collectives  77.3 us (93%)
  Pallas kernels  4.27 us (5%)
  local copies, waits for them, and re-layouts  0.94 us (1%)
    all_to_all x1, blocking collectives, body(): lax.all_to_all(packed.reshape(blocks_a, 1, total * 128), GA, split_axis=0...  30.2 us
    all_to_all x1, blocking collectives, body(): got = lax.all_to_all(back, RANKS, split_axis=0, concat_axis=0, tiled=True)  26.7 us
    all_to_all x1, blocking collectives, body(): got = lax.all_to_all(sent, COL, split_axis=0, concat_axis=0, tiled=True)  20.4 us
    pallas_call x4, Pallas kernels, call(): pl.pallas_call(kernel, out_shape=jax.ShapeDtypeStruct(shape, jnp.float32)...  4.27 us

profile of v4, /device:TPU:1, one launch (start us, length us, event | category | flops | bytes accessed | tf_op | source)
XLA Modules:
  0.0 82.6 jit_solution(15421673884759005206)
XLA Ops:
  0.0 0.0 copy-start.2
  0.0 0.9 %copy-done.2 = f32[8,16,256]{2,1,0:T(8,128)S(1)} copy-done((f32[8,16,256]{2,1,0:T(8,128)S(1)}, f32[8,16,256]{2,1,0:T(8,128)}, u32[]{:S(2)}) %copy-start.2) | copy-done | bytes 131096
  0.9 0.0 copy-start
  0.9 0.6 shard_map.73
  1.5 20.4 %all_to_all.27 = f32[16,32,128]{2,1,0:T(8,128)S(1)} all-to-all(f32[16,32,128]{2,1,0:T(8,128)S(1)} %bitcast.13), channel_id=1, replica_groups=mesh['grp'=2,'ra'=8,'rb'=2,'ca'=2,'cb'=8] {'ca','cb'}, dimensions={0} | all-to-all | bytes 524288 | tf_op jit(solution)/shard_map/all_to_all | solution.py:242
  21.9 0.0 copy-done
  21.9 0.0 copy-start.5
  21.9 0.0 copy-start.6
  21.9 0.4 shard_map.74
  22.4 0.0 copy-start.3
  22.4 0.0 copy-start.4
  22.4 30.2 %all_to_all.28 = f32[32,1,4352]{2,1,0:T(1,128)S(1)} all-to-all(f32[32,1,4352]{2,1,0:T(1,128)S(1)} %bitcast.8), channel_id=1, replica_groups=mesh['grp'=2,'ra'=8,'rb'=2,'ca'=2,'cb'=8] {'grp','ra','rb'}, dimensions={0} | all-to-all | bytes 1114112 | tf_op jit(solution)/shard_map/all_to_all | solution.py:244
  52.5 0.0 copy-done.5
  52.6 0.0 copy-done.6
  52.6 0.0 copy-done.3
  52.6 0.0 copy-done.4
  52.6 2.3 %shard_map.75 = f32[512,128]{1,0:T(8,128)S(1)} custom-call(f32[1088,128]{1,0:T(8,128)S(1)} %bitcast.11, bf16[2,256,512]{2,1,0:T(8,128)(2,1)S(1)} %copy-done.6, bf16[2,512,256]{2,1,0:T(8,128)(2,1)S(1)} %copy-done.4, bf16[2,512,256]{2,1,0:T(8,128)(2,1)S(1)} %copy-done.5, bf16[2,256,512]{2,1,0:T(8,128)(2,1)S(1)} %copy-done.3), custom_call_target="tpu_custom_call" | custom-call | flops 1200000000 | bytes 2916352 | tf_op jit(solution)/shard_map/pallas_call | solution.py:196
  54.8 0.0 copy-start.1
  54.9 26.7 %all_to_all.29 = f32[512,1,128]{2,1,0:T(1,128)S(1)} all-to-all(f32[512,1,128]{2,1,0:T(1,128)S(1)} %bitcast.12), channel_id=1, replica_groups=mesh['grp'=2,'ra'=8,'rb'=2,'ca'=2,'cb'=8] {'grp','cb','ra','rb','ca'}, dimensions={0} | all-to-all | bytes 524288 | tf_op jit(solution)/shard_map/all_to_all | solution.py:251
  81.6 0.0 copy-done.1
  81.6 1.0 %shard_map.76 = f32[8,16,256]{2,1,0:T(8,128)} custom-call(f32[512,128]{1,0:T(8,128)S(1)} %bitcast.9, bf16[2,512,256]{2,1,0:T(8,128)(2,1)S(1)} %copy-done.1), custom_call_target="tpu_custom_call" | custom-call | flops 100663296 | bytes 917504 | tf_op jit(solution)/shard_map/pallas_call | solution.py:196
Async XLA Ops:
  0.0 0.9 %copy-start.2 = (f32[8,16,256]{2,1,0:T(8,128)S(1)}, f32[8,16,256]{2,1,0:T(8,128)}, u32[]{:S(2)}) copy-start(f32[8,16,256]{2,1,0:T(8,128)} %d_ref.1) | copy-start | bytes 393220
  0.9 21.0 %copy-start = (f32[16,32,512]{2,1,0:T(8,128)S(1)}, f32[16,32,512]{2,1,0:T(8,128)}, u32[]{:S(2)}) copy-start(f32[16,32,512]{2,1,0:T(8,128)} %k_ref.1) | copy-start | bytes 3145732
  21.9 30.6 %copy-start.5 = (bf16[2,512,256]{2,1,0:T(8,128)(2,1)S(1)}, bf16[2,512,256]{2,1,0:T(8,128)(2,1)}, u32[]{:S(2)}) copy-start(bf16[2,512,256]{2,1,0:T(8,128)(2,1)} %constant.12.clone.y_back_ref) | copy-start | bytes 1572868
  21.9 30.6 %copy-start.6 = (bf16[2,256,512]{2,1,0:T(8,128)(2,1)S(1)}, bf16[2,256,512]{2,1,0:T(8,128)(2,1)}, u32[]{:S(2)}) copy-start(bf16[2,256,512]{2,1,0:T(8,128)(2,1)} %constant.11.clone.y_ref) | copy-start | bytes 1572868
  22.4 30.2 %copy-start.3 = (bf16[2,256,512]{2,1,0:T(8,128)(2,1)S(1)}, bf16[2,256,512]{2,1,0:T(8,128)(2,1)}, u32[]{:S(2)}) copy-start(bf16[2,256,512]{2,1,0:T(8,128)(2,1)} %constant.14.clone.x_back_ref) | copy-start | bytes 1572868
  22.4 30.2 %copy-start.4 = (bf16[2,512,256]{2,1,0:T(8,128)(2,1)S(1)}, bf16[2,512,256]{2,1,0:T(8,128)(2,1)}, u32[]{:S(2)}) copy-start(bf16[2,512,256]{2,1,0:T(8,128)(2,1)} %constant.13.clone.x_ref) | copy-start | bytes 1572868
  54.8 26.7 %copy-start.1 = (bf16[2,512,256]{2,1,0:T(8,128)(2,1)S(1)}, bf16[2,512,256]{2,1,0:T(8,128)(2,1)}, u32[]{:S(2)}) copy-start(bf16[2,512,256]{2,1,0:T(8,128)(2,1)} %constant.10.clone.t_ref) | copy-start | bytes 1572868

commit v5 on v4

--- a/solution.py
+++ b/solution.py
@@ -14,7 +14,7 @@
 
 GA = ("grp", "ra", "rb")
 COL = ("ca", "cb")
-RANKS = ("grp", "cb", "ra", "rb", "ca")
+RANKS = ("grp", "ra", "cb", "ca", "rb")
 NN = (((1,), (0,)), ((), ()))
 NT = (((1,), (1,)), ((), ()))
 VMEM = pl.BlockSpec(memory_space=pltpu.VMEM)

time: 82.8 us -> 82.4 us (level)
  no operation moved by 1% of the time
where the time goes in v5:
time: 82.4 us; the launch traced here: 82.2 us
  blocking collectives  76.9 us (93%)
  Pallas kernels  4.28 us (5%)
  local copies, waits for them, and re-layouts  0.94 us (1%)
    all_to_all x1, blocking collectives, body(): lax.all_to_all(packed.reshape(blocks_a, 1, total * 128), GA, split_axis=0...  30.2 us
    all_to_all x1, blocking collectives, body(): got = lax.all_to_all(back, RANKS, split_axis=0, concat_axis=0, tiled=True)  26.3 us
    all_to_all x1, blocking collectives, body(): got = lax.all_to_all(sent, COL, split_axis=0, concat_axis=0, tiled=True)  20.4 us
    pallas_call x4, Pallas kernels, call(): pl.pallas_call(kernel, out_shape=jax.ShapeDtypeStruct(shape, jnp.float32)...  4.28 us

profile of v5, /device:TPU:1, one launch (start us, length us, event | category | flops | bytes accessed | tf_op | source)
XLA Modules:
  0.0 82.2 jit_solution(7800240327193791057)
XLA Ops:
  0.0 0.0 copy-start.2
  0.0 0.9 %copy-done.2 = f32[8,16,256]{2,1,0:T(8,128)S(1)} copy-done((f32[8,16,256]{2,1,0:T(8,128)S(1)}, f32[8,16,256]{2,1,0:T(8,128)}, u32[]{:S(2)}) %copy-start.2) | copy-done | bytes 131096
  0.9 0.0 copy-start
  0.9 0.6 shard_map.73
  1.5 20.4 %all_to_all.27 = f32[16,32,128]{2,1,0:T(8,128)S(1)} all-to-all(f32[16,32,128]{2,1,0:T(8,128)S(1)} %bitcast.13), channel_id=1, replica_groups=mesh['grp'=2,'ra'=8,'rb'=2,'ca'=2,'cb'=8] {'ca','cb'}, dimensions={0} | all-to-all | bytes 524288 | tf_op jit(solution)/shard_map/all_to_all | solution.py:242
  21.9 0.0 copy-done
  21.9 0.0 copy-start.5
  21.9 0.0 copy-start.6
  21.9 0.4 shard_map.74
  22.4 0.0 copy-start.3
  22.4 0.0 copy-start.4
  22.4 30.2 %all_to_all.28 = f32[32,1,4352]{2,1,0:T(1,128)S(1)} all-to-all(f32[32,1,4352]{2,1,0:T(1,128)S(1)} %bitcast.8), channel_id=1, replica_groups=mesh['grp'=2,'ra'=8,'rb'=2,'ca'=2,'cb'=8] {'grp','ra','rb'}, dimensions={0} | all-to-all | bytes 1114112 | tf_op jit(solution)/shard_map/all_to_all | solution.py:244
  52.5 0.0 copy-done.5
  52.6 0.0 copy-done.6
  52.6 0.0 copy-done.3
  52.6 0.0 copy-done.4
  52.6 2.3 %shard_map.75 = f32[512,128]{1,0:T(8,128)S(1)} custom-call(f32[1088,128]{1,0:T(8,128)S(1)} %bitcast.11, bf16[2,256,512]{2,1,0:T(8,128)(2,1)S(1)} %copy-done.6, bf16[2,512,256]{2,1,0:T(8,128)(2,1)S(1)} %copy-done.4, bf16[2,512,256]{2,1,0:T(8,128)(2,1)S(1)} %copy-done.5, bf16[2,256,512]{2,1,0:T(8,128)(2,1)S(1)} %copy-done.3), custom_call_target="tpu_custom_call" | custom-call | flops 1200000000 | bytes 2916352 | tf_op jit(solution)/shard_map/pallas_call | solution.py:196
  54.9 0.0 copy-start.1
  54.9 26.3 %all_to_all.29 = f32[512,1,128]{2,1,0:T(1,128)S(1)} all-to-all(f32[512,1,128]{2,1,0:T(1,128)S(1)} %bitcast.12), channel_id=1, replica_groups=mesh['grp'=2,'ra'=8,'rb'=2,'ca'=2,'cb'=8] {'grp','ra','cb','ca','rb'}, dimensions={0} | all-to-all | bytes 524288 | tf_op jit(solution)/shard_map/all_to_all | solution.py:251
  81.2 0.0 copy-done.1
  81.2 1.0 %shard_map.76 = f32[8,16,256]{2,1,0:T(8,128)} custom-call(f32[512,128]{1,0:T(8,128)S(1)} %bitcast.9, bf16[2,512,256]{2,1,0:T(8,128)(2,1)S(1)} %copy-done.1), custom_call_target="tpu_custom_call" | custom-call | flops 100663296 | bytes 917504 | tf_op jit(solution)/shard_map/pallas_call | solution.py:196
Async XLA Ops:
  0.0 0.9 %copy-start.2 = (f32[8,16,256]{2,1,0:T(8,128)S(1)}, f32[8,16,256]{2,1,0:T(8,128)}, u32[]{:S(2)}) copy-start(f32[8,16,256]{2,1,0:T(8,128)} %d_ref.1) | copy-start | bytes 393220
  0.9 21.0 %copy-start = (f32[16,32,512]{2,1,0:T(8,128)S(1)}, f32[16,32,512]{2,1,0:T(8,128)}, u32[]{:S(2)}) copy-start(f32[16,32,512]{2,1,0:T(8,128)} %k_ref.1) | copy-start | bytes 3145732
  21.9 30.6 %copy-start.5 = (bf16[2,512,256]{2,1,0:T(8,128)(2,1)S(1)}, bf16[2,512,256]{2,1,0:T(8,128)(2,1)}, u32[]{:S(2)}) copy-start(bf16[2,512,256]{2,1,0:T(8,128)(2,1)} %constant.12.clone.y_back_ref) | copy-start | bytes 1572868
  21.9 30.6 %copy-start.6 = (bf16[2,256,512]{2,1,0:T(8,128)(2,1)S(1)}, bf16[2,256,512]{2,1,0:T(8,128)(2,1)}, u32[]{:S(2)}) copy-start(bf16[2,256,512]{2,1,0:T(8,128)(2,1)} %constant.11.clone.y_ref) | copy-start | bytes 1572868
  22.4 30.2 %copy-start.3 = (bf16[2,256,512]{2,1,0:T(8,128)(2,1)S(1)}, bf16[2,256,512]{2,1,0:T(8,128)(2,1)}, u32[]{:S(2)}) copy-start(bf16[2,256,512]{2,1,0:T(8,128)(2,1)} %constant.14.clone.x_back_ref) | copy-start | bytes 1572868
  22.4 30.2 %copy-start.4 = (bf16[2,512,256]{2,1,0:T(8,128)(2,1)S(1)}, bf16[2,512,256]{2,1,0:T(8,128)(2,1)}, u32[]{:S(2)}) copy-start(bf16[2,512,256]{2,1,0:T(8,128)(2,1)} %constant.13.clone.x_ref) | copy-start | bytes 1572868
  54.9 26.3 %copy-start.1 = (bf16[2,512,256]{2,1,0:T(8,128)(2,1)S(1)}, bf16[2,512,256]{2,1,0:T(8,128)(2,1)}, u32[]{:S(2)}) copy-start(bf16[2,512,256]{2,1,0:T(8,128)(2,1)} %constant.10.clone.t_ref) | copy-start | bytes 1572868

commit v6 on v5

--- a/solution.py
+++ b/solution.py
@@ -128,6 +128,8 @@
     r = jnp.concatenate(
         [jnp.concatenate([take(h * per + n) for n in range(per)], 0) for h in range(blocks_b // per)], 1
     )
+    p = split(dot3(split(r), (y_ref[0], y_ref[1]), NN))
+    q0 = [dot3((x_ref[0, at], x_ref[1, at]), p, NN) for at in (slice(0, half), slice(half, 2 * half))]
     spare, middle = blocks_b + rows * tiles, blocks_a // 2
 
     def kernel_tile(s, h):
@@ -156,13 +158,10 @@
         jnp.concatenate([main, jnp.where(first_lane, column, main)], 1),
         jnp.concatenate([lined, jnp.where(first_lane, with_column, lined)], 1),
     )
-    p = split(dot3(split(r), (y_ref[0], y_ref[1]), NN))
     y_back = (y_back_ref[0], y_back_ref[1])
     u = []
     for part in range(2):
-        at = slice(part * half, (part + 1) * half)
-        q = dot3((x_ref[0, at], x_ref[1, at]), p, NN) * kernels[part]
-        u.append(dot3(split(q), y_back, NN))
+        u.append(dot3(split(q0[part] * kernels[part]), y_back, NN))
     v = dot3((x_back_ref[0], x_back_ref[1]), split(jnp.concatenate(u, 0)), NN)
     for h in range(blocks_b // per):
         lanes = slice(h * per * slab_y, (h + 1) * per * slab_y)

time: 82.4 us -> 82.3 us (level)
  no operation moved by 1% of the time
where the time goes in v6:
time: 82.3 us; the launch traced here: 82 us
  blocking collectives  76.9 us (93%)
  Pallas kernels  4.18 us (5%)
  local copies, waits for them, and re-layouts  0.94 us (1%)
    all_to_all x1, blocking collectives, body(): lax.all_to_all(packed.reshape(blocks_a, 1, total * 128), GA, split_axis=0...  30.2 us
    all_to_all x1, blocking collectives, body(): got = lax.all_to_all(back, RANKS, split_axis=0, concat_axis=0, tiled=True)  26.3 us
    all_to_all x1, blocking collectives, body(): got = lax.all_to_all(sent, COL, split_axis=0, concat_axis=0, tiled=True)  20.4 us
    pallas_call x4, Pallas kernels, call(): pl.pallas_call(kernel, out_shape=jax.ShapeDtypeStruct(shape, jnp.float32)...  4.18 us

profile of v6, /device:TPU:1, one launch (start us, length us, event | category | flops | bytes accessed | tf_op | source)
XLA Modules:
  0.0 82.0 jit_solution(18149584232388069854)
XLA Ops:
  0.0 0.0 copy-start.2
  0.0 0.9 %copy-done.2 = f32[8,16,256]{2,1,0:T(8,128)S(1)} copy-done((f32[8,16,256]{2,1,0:T(8,128)S(1)}, f32[8,16,256]{2,1,0:T(8,128)}, u32[]{:S(2)}) %copy-start.2) | copy-done | bytes 131096
  0.9 0.0 copy-start
  0.9 0.6 shard_map.73
  1.5 20.4 %all_to_all.27 = f32[16,32,128]{2,1,0:T(8,128)S(1)} all-to-all(f32[16,32,128]{2,1,0:T(8,128)S(1)} %bitcast.13), channel_id=1, replica_groups=mesh['grp'=2,'ra'=8,'rb'=2,'ca'=2,'cb'=8] {'ca','cb'}, dimensions={0} | all-to-all | bytes 524288 | tf_op jit(solution)/shard_map/all_to_all | solution.py:241
  21.9 0.0 copy-done
  21.9 0.0 copy-start.5
  21.9 0.0 copy-start.6
  21.9 0.4 shard_map.74
  22.4 0.0 copy-start.3
  22.4 0.0 copy-start.4
  22.4 30.2 %all_to_all.28 = f32[32,1,4352]{2,1,0:T(1,128)S(1)} all-to-all(f32[32,1,4352]{2,1,0:T(1,128)S(1)} %bitcast.8), channel_id=1, replica_groups=mesh['grp'=2,'ra'=8,'rb'=2,'ca'=2,'cb'=8] {'grp','ra','rb'}, dimensions={0} | all-to-all | bytes 1114112 | tf_op jit(solution)/shard_map/all_to_all | solution.py:243
  52.5 0.0 copy-done.5
  52.6 0.0 copy-done.6
  52.6 0.0 copy-done.3
  52.6 0.0 copy-done.4
  52.6 2.2 %shard_map.75 = f32[512,128]{1,0:T(8,128)S(1)} custom-call(f32[1088,128]{1,0:T(8,128)S(1)} %bitcast.11, bf16[2,256,512]{2,1,0:T(8,128)(2,1)S(1)} %copy-done.6, bf16[2,512,256]{2,1,0:T(8,128)(2,1)S(1)} %copy-done.4, bf16[2,512,256]{2,1,0:T(8,128)(2,1)S(1)} %copy-done.5, bf16[2,256,512]{2,1,0:T(8,128)(2,1)S(1)} %copy-done.3), custom_call_target="tpu_custom_call" | custom-call | flops 1200000000 | bytes 2916352 | tf_op jit(solution)/shard_map/pallas_call | solution.py:195
  54.8 0.0 copy-start.1
  54.8 26.3 %all_to_all.29 = f32[512,1,128]{2,1,0:T(1,128)S(1)} all-to-all(f32[512,1,128]{2,1,0:T(1,128)S(1)} %bitcast.12), channel_id=1, replica_groups=mesh['grp'=2,'ra'=8,'rb'=2,'ca'=2,'cb'=8] {'grp','ra','cb','ca','rb'}, dimensions={0} | all-to-all | bytes 524288 | tf_op jit(solution)/shard_map/all_to_all | solution.py:250
  81.1 0.0 copy-done.1
  81.1 1.0 %shard_map.76 = f32[8,16,256]{2,1,0:T(8,128)} custom-call(f32[512,128]{1,0:T(8,128)S(1)} %bitcast.9, bf16[2,512,256]{2,1,0:T(8,128)(2,1)S(1)} %copy-done.1), custom_call_target="tpu_custom_call" | custom-call | flops 100663296 | bytes 917504 | tf_op jit(solution)/shard_map/pallas_call | solution.py:195
Async XLA Ops:
  0.0 0.9 %copy-start.2 = (f32[8,16,256]{2,1,0:T(8,128)S(1)}, f32[8,16,256]{2,1,0:T(8,128)}, u32[]{:S(2)}) copy-start(f32[8,16,256]{2,1,0:T(8,128)} %d_ref.1) | copy-start | bytes 393220
  0.9 21.0 %copy-start = (f32[16,32,512]{2,1,0:T(8,128)S(1)}, f32[16,32,512]{2,1,0:T(8,128)}, u32[]{:S(2)}) copy-start(f32[16,32,512]{2,1,0:T(8,128)} %k_ref.1) | copy-start | bytes 3145732
  21.9 30.6 %copy-start.5 = (bf16[2,512,256]{2,1,0:T(8,128)(2,1)S(1)}, bf16[2,512,256]{2,1,0:T(8,128)(2,1)}, u32[]{:S(2)}) copy-start(bf16[2,512,256]{2,1,0:T(8,128)(2,1)} %constant.12.clone.y_back_ref) | copy-start | bytes 1572868
  21.9 30.6 %copy-start.6 = (bf16[2,256,512]{2,1,0:T(8,128)(2,1)S(1)}, bf16[2,256,512]{2,1,0:T(8,128)(2,1)}, u32[]{:S(2)}) copy-start(bf16[2,256,512]{2,1,0:T(8,128)(2,1)} %constant.11.clone.y_ref) | copy-start | bytes 1572868
  22.4 30.2 %copy-start.3 = (bf16[2,256,512]{2,1,0:T(8,128)(2,1)S(1)}, bf16[2,256,512]{2,1,0:T(8,128)(2,1)}, u32[]{:S(2)}) copy-start(bf16[2,256,512]{2,1,0:T(8,128)(2,1)} %constant.14.clone.x_back_ref) | copy-start | bytes 1572868
  22.4 30.2 %copy-start.4 = (bf16[2,512,256]{2,1,0:T(8,128)(2,1)S(1)}, bf16[2,512,256]{2,1,0:T(8,128)(2,1)}, u32[]{:S(2)}) copy-start(bf16[2,512,256]{2,1,0:T(8,128)(2,1)} %constant.13.clone.x_ref) | copy-start | bytes 1572868
  54.8 26.3 %copy-start.1 = (bf16[2,512,256]{2,1,0:T(8,128)(2,1)S(1)}, bf16[2,512,256]{2,1,0:T(8,128)(2,1)}, u32[]{:S(2)}) copy-start(bf16[2,512,256]{2,1,0:T(8,128)(2,1)} %constant.10.clone.t_ref) | copy-start | bytes 1572868

commit v7 on v6

--- a/solution.py
+++ b/solution.py
@@ -17,6 +17,7 @@
 RANKS = ("grp", "ra", "cb", "ca", "rb")
 NN = (((1,), (0,)), ((), ()))
 NT = (((1,), (1,)), ((), ()))
+TN = (((0,), (0,)), ((), ()))
 VMEM = pl.BlockSpec(memory_space=pltpu.VMEM)
 
 
@@ -174,7 +175,7 @@
 
 
 def inverse_z(r_ref, t_ref, out_ref):
-    out = dot3(split(r_ref[...].T), (t_ref[0], t_ref[1]), NN)
+    out = dot3(split(r_ref[...]), (t_ref[0], t_ref[1]), TN)
     out_ref[...] = out.reshape(out_ref.shape)
 
 

time: 82.3 us -> 82.3 us (level)
  no operation moved by 1% of the time
where the time goes in v7:
time: 82.3 us; the launch traced here: 82 us
  blocking collectives  76.9 us (93%)
  Pallas kernels  4.16 us (5%)
  local copies, waits for them, and re-layouts  0.94 us (1%)
    all_to_all x1, blocking collectives, body(): lax.all_to_all(packed.reshape(blocks_a, 1, total * 128), GA, split_axis=0...  30.2 us
    all_to_all x1, blocking collectives, body(): got = lax.all_to_all(back, RANKS, split_axis=0, concat_axis=0, tiled=True)  26.3 us
    all_to_all x1, blocking collectives, body(): got = lax.all_to_all(sent, COL, split_axis=0, concat_axis=0, tiled=True)  20.4 us
    pallas_call x4, Pallas kernels, call(): pl.pallas_call(kernel, out_shape=jax.ShapeDtypeStruct(shape, jnp.float32)...  4.16 us

profile of v7, /device:TPU:1, one launch (start us, length us, event | category | flops | bytes accessed | tf_op | source)
XLA Modules:
  0.0 82.0 jit_solution(18347335836043356300)
XLA Ops:
  0.0 0.0 copy-start.2
  0.0 0.9 %copy-done.2 = f32[8,16,256]{2,1,0:T(8,128)S(1)} copy-done((f32[8,16,256]{2,1,0:T(8,128)S(1)}, f32[8,16,256]{2,1,0:T(8,128)}, u32[]{:S(2)}) %copy-start.2) | copy-done | bytes 131096
  0.9 0.0 copy-start
  0.9 0.6 shard_map.73
  1.5 20.4 %all_to_all.27 = f32[16,32,128]{2,1,0:T(8,128)S(1)} all-to-all(f32[16,32,128]{2,1,0:T(8,128)S(1)} %bitcast.13), channel_id=1, replica_groups=mesh['grp'=2,'ra'=8,'rb'=2,'ca'=2,'cb'=8] {'ca','cb'}, dimensions={0} | all-to-all | bytes 524288 | tf_op jit(solution)/shard_map/all_to_all | solution.py:242
  21.9 0.0 copy-done
  21.9 0.0 copy-start.5
  21.9 0.0 copy-start.6
  21.9 0.4 shard_map.74
  22.4 0.0 copy-start.3
  22.4 0.0 copy-start.4
  22.4 30.2 %all_to_all.28 = f32[32,1,4352]{2,1,0:T(1,128)S(1)} all-to-all(f32[32,1,4352]{2,1,0:T(1,128)S(1)} %bitcast.8), channel_id=1, replica_groups=mesh['grp'=2,'ra'=8,'rb'=2,'ca'=2,'cb'=8] {'grp','ra','rb'}, dimensions={0} | all-to-all | bytes 1114112 | tf_op jit(solution)/shard_map/all_to_all | solution.py:244
  52.5 0.0 copy-done.5
  52.6 0.0 copy-done.6
  52.6 0.0 copy-done.3
  52.6 0.0 copy-done.4
  52.6 2.2 %shard_map.75 = f32[512,128]{1,0:T(8,128)S(1)} custom-call(f32[1088,128]{1,0:T(8,128)S(1)} %bitcast.11, bf16[2,256,512]{2,1,0:T(8,128)(2,1)S(1)} %copy-done.6, bf16[2,512,256]{2,1,0:T(8,128)(2,1)S(1)} %copy-done.4, bf16[2,512,256]{2,1,0:T(8,128)(2,1)S(1)} %copy-done.5, bf16[2,256,512]{2,1,0:T(8,128)(2,1)S(1)} %copy-done.3), custom_call_target="tpu_custom_call" | custom-call | flops 1200000000 | bytes 2916352 | tf_op jit(solution)/shard_map/pallas_call | solution.py:196
  54.8 0.0 copy-start.1
  54.8 26.3 %all_to_all.29 = f32[512,1,128]{2,1,0:T(1,128)S(1)} all-to-all(f32[512,1,128]{2,1,0:T(1,128)S(1)} %bitcast.12), channel_id=1, replica_groups=mesh['grp'=2,'ra'=8,'rb'=2,'ca'=2,'cb'=8] {'grp','ra','cb','ca','rb'}, dimensions={0} | all-to-all | bytes 524288 | tf_op jit(solution)/shard_map/all_to_all | solution.py:251
  81.1 0.0 copy-done.1
  81.1 1.0 %shard_map.76 = f32[8,16,256]{2,1,0:T(8,128)} custom-call(f32[512,128]{1,0:T(8,128)S(1)} %bitcast.9, bf16[2,512,256]{2,1,0:T(8,128)(2,1)S(1)} %copy-done.1), custom_call_target="tpu_custom_call" | custom-call | flops 100663296 | bytes 917504 | tf_op jit(solution)/shard_map/pallas_call | solution.py:196
Async XLA Ops:
  0.0 0.9 %copy-start.2 = (f32[8,16,256]{2,1,0:T(8,128)S(1)}, f32[8,16,256]{2,1,0:T(8,128)}, u32[]{:S(2)}) copy-start(f32[8,16,256]{2,1,0:T(8,128)} %d_ref.1) | copy-start | bytes 393220
  0.9 21.0 %copy-start = (f32[16,32,512]{2,1,0:T(8,128)S(1)}, f32[16,32,512]{2,1,0:T(8,128)}, u32[]{:S(2)}) copy-start(f32[16,32,512]{2,1,0:T(8,128)} %k_ref.1) | copy-start | bytes 3145732
  21.9 30.6 %copy-start.5 = (bf16[2,512,256]{2,1,0:T(8,128)(2,1)S(1)}, bf16[2,512,256]{2,1,0:T(8,128)(2,1)}, u32[]{:S(2)}) copy-start(bf16[2,512,256]{2,1,0:T(8,128)(2,1)} %constant.12.clone.y_back_ref) | copy-start | bytes 1572868
  21.9 30.6 %copy-start.6 = (bf16[2,256,512]{2,1,0:T(8,128)(2,1)S(1)}, bf16[2,256,512]{2,1,0:T(8,128)(2,1)}, u32[]{:S(2)}) copy-start(bf16[2,256,512]{2,1,0:T(8,128)(2,1)} %constant.11.clone.y_ref) | copy-start | bytes 1572868
  22.4 30.2 %copy-start.3 = (bf16[2,256,512]{2,1,0:T(8,128)(2,1)S(1)}, bf16[2,256,512]{2,1,0:T(8,128)(2,1)}, u32[]{:S(2)}) copy-start(bf16[2,256,512]{2,1,0:T(8,128)(2,1)} %constant.14.clone.x_back_ref) | copy-start | bytes 1572868
  22.4 30.2 %copy-start.4 = (bf16[2,512,256]{2,1,0:T(8,128)(2,1)S(1)}, bf16[2,512,256]{2,1,0:T(8,128)(2,1)}, u32[]{:S(2)}) copy-start(bf16[2,512,256]{2,1,0:T(8,128)(2,1)} %constant.13.clone.x_ref) | copy-start | bytes 1572868
  54.8 26.3 %copy-start.1 = (bf16[2,512,256]{2,1,0:T(8,128)(2,1)S(1)}, bf16[2,512,256]{2,1,0:T(8,128)(2,1)}, u32[]{:S(2)}) copy-start(bf16[2,512,256]{2,1,0:T(8,128)(2,1)} %constant.10.clone.t_ref) | copy-start | bytes 1572868

commit v8 on v6

--- a/solution.py
+++ b/solution.py
@@ -14,7 +14,7 @@
 
 GA = ("grp", "ra", "rb")
 COL = ("ca", "cb")
-RANKS = ("grp", "ra", "cb", "ca", "rb")
+RANKS = ("cb", "ra", "ca", "rb", "grp")
 NN = (((1,), (0,)), ((), ()))
 NT = (((1,), (1,)), ((), ()))
 VMEM = pl.BlockSpec(memory_space=pltpu.VMEM)

time: 82.3 us -> 82.1 us (level)
  no operation moved by 1% of the time
where the time goes in v8:
time: 82.1 us; the launch traced here: 81.9 us
  blocking collectives  76.7 us (93%)
  Pallas kernels  4.17 us (5%)
  local copies, waits for them, and re-layouts  0.94 us (1%)
    all_to_all x1, blocking collectives, body(): lax.all_to_all(packed.reshape(blocks_a, 1, total * 128), GA, split_axis=0...  30.2 us
    all_to_all x1, blocking collectives, body(): got = lax.all_to_all(back, RANKS, split_axis=0, concat_axis=0, tiled=True)  26.1 us
    all_to_all x1, blocking collectives, body(): got = lax.all_to_all(sent, COL, split_axis=0, concat_axis=0, tiled=True)  20.4 us
    pallas_call x4, Pallas kernels, call(): pl.pallas_call(kernel, out_shape=jax.ShapeDtypeStruct(shape, jnp.float32)...  4.17 us

profile of v8, /device:TPU:1, one launch (start us, length us, event | category | flops | bytes accessed | tf_op | source)
XLA Modules:
  0.0 81.9 jit_solution(2165994242914869874)
XLA Ops:
  0.0 0.0 copy-start.2
  0.0 0.9 %copy-done.2 = f32[8,16,256]{2,1,0:T(8,128)S(1)} copy-done((f32[8,16,256]{2,1,0:T(8,128)S(1)}, f32[8,16,256]{2,1,0:T(8,128)}, u32[]{:S(2)}) %copy-start.2) | copy-done | bytes 131096
  0.9 0.0 copy-start
  0.9 0.6 shard_map.73
  1.5 20.4 %all_to_all.27 = f32[16,32,128]{2,1,0:T(8,128)S(1)} all-to-all(f32[16,32,128]{2,1,0:T(8,128)S(1)} %bitcast.13), channel_id=1, replica_groups=mesh['grp'=2,'ra'=8,'rb'=2,'ca'=2,'cb'=8] {'ca','cb'}, dimensions={0} | all-to-all | bytes 524288 | tf_op jit(solution)/shard_map/all_to_all | solution.py:241
  21.9 0.0 copy-done
  21.9 0.0 copy-start.5
  21.9 0.0 copy-start.6
  21.9 0.4 shard_map.74
  22.4 0.0 copy-start.3
  22.4 0.0 copy-start.4
  22.4 30.2 %all_to_all.28 = f32[32,1,4352]{2,1,0:T(1,128)S(1)} all-to-all(f32[32,1,4352]{2,1,0:T(1,128)S(1)} %bitcast.8), channel_id=1, replica_groups=mesh['grp'=2,'ra'=8,'rb'=2,'ca'=2,'cb'=8] {'grp','ra','rb'}, dimensions={0} | all-to-all | bytes 1114112 | tf_op jit(solution)/shard_map/all_to_all | solution.py:243
  52.5 0.0 copy-done.5
  52.6 0.0 copy-done.6
  52.6 0.0 copy-done.3
  52.6 0.0 copy-done.4
  52.6 2.2 %shard_map.75 = f32[512,128]{1,0:T(8,128)S(1)} custom-call(f32[1088,128]{1,0:T(8,128)S(1)} %bitcast.11, bf16[2,256,512]{2,1,0:T(8,128)(2,1)S(1)} %copy-done.6, bf16[2,512,256]{2,1,0:T(8,128)(2,1)S(1)} %copy-done.4, bf16[2,512,256]{2,1,0:T(8,128)(2,1)S(1)} %copy-done.5, bf16[2,256,512]{2,1,0:T(8,128)(2,1)S(1)} %copy-done.3), custom_call_target="tpu_custom_call" | custom-call | flops 1200000000 | bytes 2916352 | tf_op jit(solution)/shard_map/pallas_call | solution.py:195
  54.8 0.0 copy-start.1
  54.8 26.1 %all_to_all.29 = f32[512,1,128]{2,1,0:T(1,128)S(1)} all-to-all(f32[512,1,128]{2,1,0:T(1,128)S(1)} %bitcast.12), channel_id=1, replica_groups=mesh['grp'=2,'ra'=8,'rb'=2,'ca'=2,'cb'=8] {'cb','ra','ca','rb','grp'}, dimensions={0} | all-to-all | bytes 524288 | tf_op jit(solution)/shard_map/all_to_all | solution.py:250
  80.9 0.0 copy-done.1
  80.9 1.0 %shard_map.76 = f32[8,16,256]{2,1,0:T(8,128)} custom-call(f32[512,128]{1,0:T(8,128)S(1)} %bitcast.9, bf16[2,512,256]{2,1,0:T(8,128)(2,1)S(1)} %copy-done.1), custom_call_target="tpu_custom_call" | custom-call | flops 100663296 | bytes 917504 | tf_op jit(solution)/shard_map/pallas_call | solution.py:195
Async XLA Ops:
  0.0 0.9 %copy-start.2 = (f32[8,16,256]{2,1,0:T(8,128)S(1)}, f32[8,16,256]{2,1,0:T(8,128)}, u32[]{:S(2)}) copy-start(f32[8,16,256]{2,1,0:T(8,128)} %d_ref.1) | copy-start | bytes 393220
  0.9 21.0 %copy-start = (f32[16,32,512]{2,1,0:T(8,128)S(1)}, f32[16,32,512]{2,1,0:T(8,128)}, u32[]{:S(2)}) copy-start(f32[16,32,512]{2,1,0:T(8,128)} %k_ref.1) | copy-start | bytes 3145732
  21.9 30.6 %copy-start.5 = (bf16[2,512,256]{2,1,0:T(8,128)(2,1)S(1)}, bf16[2,512,256]{2,1,0:T(8,128)(2,1)}, u32[]{:S(2)}) copy-start(bf16[2,512,256]{2,1,0:T(8,128)(2,1)} %constant.12.clone.y_back_ref) | copy-start | bytes 1572868
  21.9 30.6 %copy-start.6 = (bf16[2,256,512]{2,1,0:T(8,128)(2,1)S(1)}, bf16[2,256,512]{2,1,0:T(8,128)(2,1)}, u32[]{:S(2)}) copy-start(bf16[2,256,512]{2,1,0:T(8,128)(2,1)} %constant.11.clone.y_ref) | copy-start | bytes 1572868
  22.4 30.2 %copy-start.3 = (bf16[2,256,512]{2,1,0:T(8,128)(2,1)S(1)}, bf16[2,256,512]{2,1,0:T(8,128)(2,1)}, u32[]{:S(2)}) copy-start(bf16[2,256,512]{2,1,0:T(8,128)(2,1)} %constant.14.clone.x_back_ref) | copy-start | bytes 1572868
  22.4 30.2 %copy-start.4 = (bf16[2,512,256]{2,1,0:T(8,128)(2,1)S(1)}, bf16[2,512,256]{2,1,0:T(8,128)(2,1)}, u32[]{:S(2)}) copy-start(bf16[2,512,256]{2,1,0:T(8,128)(2,1)} %constant.13.clone.x_ref) | copy-start | bytes 1572868
  54.8 26.1 %copy-start.1 = (bf16[2,512,256]{2,1,0:T(8,128)(2,1)S(1)}, bf16[2,512,256]{2,1,0:T(8,128)(2,1)}, u32[]{:S(2)}) copy-start(bf16[2,512,256]{2,1,0:T(8,128)(2,1)} %constant.10.clone.t_ref) | copy-start | bytes 1572868
